TPU v7x, 32 devices: a whole 2x2x4 slice. The times are simulated.
32 devices in a mesh: dp: 16 (over z, x, core), tensor: 2 (over y).
Axes of the slice: x: 2, y: 2, z: 4, core: 2. Of those that a mesh axis runs over, the one named last changes fastest.
Arguments:
- tokens: bfloat16 [32768, 512], P(('dp', 'tensor')), may hold values from -6 to 6
- segments: int32 [64, 512], P('dp'), may hold values from 0 to 7, never falling along the last dimension, each value on 1 to 256 neighbouring positions
- positions: bfloat16 [512, 512], replicated, may hold values from -3 to 3
- heads_weight: bfloat16 [512, 3, 512], P(None, None, 'tensor'), may hold values from -0.25 to 0.25
- merge_weight: bfloat16 [512, 512], P('tensor'), may hold values from -1 to 1
- merge_bias: bfloat16 [512], replicated, may hold values from -1.5 to 1.5
- first_gain: bfloat16 [512], replicated, may hold values from 0.5 to 1.5
- first_shift: bfloat16 [512], replicated, may hold values from -1.5 to 1.5
- up_weight: bfloat16 [512, 2048], P(None, 'tensor'), may hold values from -0.25 to 0.25
- up_bias: bfloat16 [2048], P('tensor'), may hold values from -2.5 to 2.5
- down_weight: bfloat16 [2048, 512], P('tensor'), may hold values from -0.1875 to 0.1875
- down_bias: bfloat16 [512], replicated, may hold values from -1.5 to 1.5
- second_gain: bfloat16 [512], replicated, may hold values from 0.5 to 1.5
- second_shift: bfloat16 [512], replicated, may hold values from -1.5 to 1.5
- cotangent: bfloat16 [32768, 512], P(('dp', 'tensor')), may hold values from -6 to 6
Outputs:
- layer_out: bfloat16 [32768, 512], P(('dp', 'tensor'))
- tokens_grad: float32 [32768, 512], P(('dp', 'tensor'))
- positions_grad: float32 [512, 512], replicated
- heads_weight_grad: float32 [512, 3, 512], P(None, None, 'tensor')
- merge_weight_grad: float32 [512, 512], P('tensor')
- merge_bias_grad: float32 [512], replicated
- first_gain_grad: float32 [512], replicated
- first_shift_grad: float32 [512], replicated
- up_weight_grad: float32 [512, 2048], P(None, 'tensor')
- up_bias_grad: float32 [2048], P('tensor')
- down_weight_grad: float32 [2048, 512], P('tensor')
- down_bias_grad: float32 [512], replicated
- second_gain_grad: float32 [512], replicated
- second_shift_grad: float32 [512], replicated
Inputs may be any that keep to these rules, and one draw needn't show every extreme that they name: `segments`: along a window the numbers never fall; no document has more than 256 characters, and in every window one has exactly that many.
All inputs are finite; a program needn't handle non-finite values.
Results may differ from a plain program's by a relative error of at most 0.013.
The roundings to bfloat16 on the way count: a program that leaves them out, or rounds other values in their place, can miss the bound.
Values may be sent and summed in bfloat16 or wider, within the bound.
A program may use at most 128 MiB of HBM per device.

v0:
```python
import jax
import jax.numpy as jnp
from jax import lax
from jax.sharding import PartitionSpec as P

HEADS = 8


def layer_norm(value, gain, shift):
    center = jnp.mean(value, -1, keepdims=True)
    centred = value - center
    spread = jnp.mean(centred * centred, -1, keepdims=True)
    return centred * lax.rsqrt(spread + 1e-05) * gain + shift


def window_scores(win_query, win_keys, win_segs, scale):
    raw = (
        jnp.einsum("thd,shd->hts", win_query, win_keys, preferred_element_type=jnp.float32) * scale
    )
    places = jnp.arange(win_segs.shape[0])
    allowed = (win_segs[:, None] == win_segs[None, :]) & (places[None, :] <= places[:, None])
    return jnp.where(allowed[None], raw, -1000000000.0)


def per_device(
    tokens,
    segments,
    positions,
    heads_weight,
    merge_weight,
    merge_bias,
    first_gain,
    first_shift,
    up_weight,
    up_bias,
    down_weight,
    down_bias,
    second_gain,
    second_shift,
    cotangent,
):
    local_rows, width = tokens.shape
    window = positions.shape[0]
    group_rows = local_rows * lax.axis_size("tensor")
    count_windows = group_rows // window
    head_size = width // HEADS
    columns = heads_weight.shape[2]
    local_heads = columns // head_size
    scale = head_size ** (-0.5)
    first_row = lax.axis_index("tensor") * local_rows
    offset = first_row % window
    copies = local_rows // window + 2
    tiled = jnp.tile(positions, (copies, 1))
    placed = lax.dynamic_slice_in_dim(tiled, offset, local_rows, 0)
    start_sum = tokens.astype(jnp.float32) + placed.astype(jnp.float32)
    attn_in = lax.all_gather(start_sum.astype(jnp.bfloat16), "tensor", axis=0, tiled=True)
    triple = jnp.einsum(
        "rd,dcf->rcf", attn_in, heads_weight, preferred_element_type=jnp.float32
    ).astype(jnp.bfloat16)
    split = triple.reshape(count_windows, window, 3, local_heads, head_size)
    query = split[:, :, 0]
    keys_all = split[:, :, 1]
    values_all = split[:, :, 2]

    def attend(items):
        win_query, win_keys, win_values, win_segs = items
        scores = window_scores(win_query, win_keys, win_segs, scale)
        peak = jnp.max(scores, -1, keepdims=True)
        expo = jnp.exp(scores - peak)
        total = jnp.sum(expo, -1, keepdims=True)
        probs = expo / total
        mixed_win = jnp.einsum(
            "hts,shd->thd",
            probs.astype(jnp.bfloat16),
            win_values,
            preferred_element_type=jnp.float32,
        )
        return (mixed_win.astype(jnp.bfloat16), (peak + jnp.log(total))[..., 0])

    mixed, log_total = lax.map(attend, (query, keys_all, values_all, segments))
    mixed_rows = mixed.reshape(group_rows, columns)
    rows_part = mixed_rows
    attn_out = lax.psum_scatter(
        jnp.dot(rows_part, merge_weight, preferred_element_type=jnp.float32),
        "tensor",
        scatter_dimension=0,
        tiled=True,
    )
    first_sum = start_sum + attn_out + merge_bias.astype(jnp.float32)
    normed, first_back = jax.vjp(
        layer_norm, first_sum, first_gain.astype(jnp.float32), first_shift.astype(jnp.float32)
    )
    ffn_in = lax.all_gather(normed.astype(jnp.bfloat16), "tensor", axis=0, tiled=True)
    pre_act = jnp.dot(ffn_in, up_weight, preferred_element_type=jnp.float32) + up_bias.astype(
        jnp.float32
    )
    hidden = jax.nn.gelu(pre_act).astype(jnp.bfloat16)
    rows_part = hidden
    branch = lax.psum_scatter(
        jnp.dot(rows_part, down_weight, preferred_element_type=jnp.float32),
        "tensor",
        scatter_dimension=0,
        tiled=True,
    )
    second_sum = normed + branch + down_bias.astype(jnp.float32)
    result, second_back = jax.vjp(
        layer_norm, second_sum, second_gain.astype(jnp.float32), second_shift.astype(jnp.float32)
    )
    layer_out = result.astype(jnp.bfloat16)
    grad_second, second_gain_grad, second_shift_grad = second_back(cotangent.astype(jnp.float32))
    down_bias_grad = jnp.sum(grad_second, 0)
    branch_grad = lax.all_gather(grad_second.astype(jnp.bfloat16), "tensor", axis=0, tiled=True)
    again, branch_grad = lax.optimization_barrier((ffn_in, branch_grad))
    pre_use = jnp.dot(again, up_weight, preferred_element_type=jnp.float32) + up_bias.astype(
        jnp.float32
    )
    hidden_use = jax.nn.gelu(pre_use).astype(jnp.bfloat16)
    down_weight_grad = jnp.einsum(
        "rf,rd->fd", hidden_use, branch_grad, preferred_element_type=jnp.float32
    )
    hidden_grad = jnp.einsum(
        "rd,fd->rf", branch_grad, down_weight, preferred_element_type=jnp.float32
    )
    _, gelu_back = jax.vjp(jax.nn.gelu, pre_use)
    pre_grad = gelu_back(hidden_grad)[0].astype(jnp.bfloat16)
    up_bias_grad = jnp.sum(pre_grad, 0, dtype=jnp.float32)
    up_weight_grad = jnp.einsum("rd,rf->df", again, pre_grad, preferred_element_type=jnp.float32)
    rows_part = pre_grad
    normed_grad = grad_second + lax.psum_scatter(
        jnp.einsum("rf,df->rd", rows_part, up_weight, preferred_element_type=jnp.float32),
        "tensor",
        scatter_dimension=0,
        tiled=True,
    )
    grad_first, first_gain_grad, first_shift_grad = first_back(normed_grad)
    merge_bias_grad = jnp.sum(grad_first, 0)
    attn_grad = lax.all_gather(grad_first.astype(jnp.bfloat16), "tensor", axis=0, tiled=True)
    merge_weight_grad = jnp.einsum(
        "rc,rd->cd", mixed_rows, attn_grad, preferred_element_type=jnp.float32
    )
    mixed_grad = jnp.einsum(
        "rd,cd->rc", attn_grad, merge_weight, preferred_element_type=jnp.float32
    )
    mixed_grad = mixed_grad.astype(jnp.bfloat16).reshape(
        count_windows, window, local_heads, head_size
    )

    def attend_back(items):
        win_query, win_keys, win_values, win_segs, win_total, win_grad = items
        scores = window_scores(win_query, win_keys, win_segs, scale)
        probs = jnp.exp(scores - win_total[..., None])
        prob_grad = jnp.einsum(
            "thd,shd->hts", win_grad, win_values, preferred_element_type=jnp.float32
        )
        inner = jnp.sum(probs * prob_grad, -1, keepdims=True)
        score_grad = (probs * (prob_grad - inner)).astype(jnp.bfloat16)
        query_grad = jnp.einsum(
            "hts,shd->thd", score_grad, win_keys, preferred_element_type=jnp.float32
        )
        key_grad = jnp.einsum(
            "hts,thd->shd", score_grad, win_query, preferred_element_type=jnp.float32
        )
        value_grad = jnp.einsum(
            "hts,thd->shd", probs.astype(jnp.bfloat16), win_grad, preferred_element_type=jnp.float32
        )
        return jnp.stack(
            [
                (query_grad * scale).astype(jnp.bfloat16),
                (key_grad * scale).astype(jnp.bfloat16),
                value_grad.astype(jnp.bfloat16),
            ],
            1,
        )

    triple_grad = lax.map(
        attend_back, (query, keys_all, values_all, segments, log_total, mixed_grad)
    )
    triple_grad = triple_grad.reshape(group_rows, 3, columns)
    heads_weight_grad = jnp.einsum(
        "rd,rcf->dcf", attn_in, triple_grad, preferred_element_type=jnp.float32
    )
    rows_part = triple_grad
    tokens_grad = grad_first + lax.psum_scatter(
        jnp.einsum(
            "rcf,dcf->rd", rows_part, heads_weight, preferred_element_type=jnp.float32
        ).astype(jnp.bfloat16),
        "tensor",
        scatter_dimension=0,
        tiled=True,
    ).astype(jnp.float32)
    canvas = jnp.zeros((copies * window, width), jnp.float32)
    canvas = lax.dynamic_update_slice_in_dim(canvas, tokens_grad, offset, 0)
    positions_grad = jnp.sum(canvas.reshape(copies, window, width), 0)
    heads_weight_grad, merge_weight_grad, up_weight_grad, up_bias_grad, down_weight_grad = lax.psum(
        (heads_weight_grad, merge_weight_grad, up_weight_grad, up_bias_grad, down_weight_grad), "dp"
    )
    (
        positions_grad,
        merge_bias_grad,
        first_gain_grad,
        first_shift_grad,
        down_bias_grad,
        second_gain_grad,
        second_shift_grad,
    ) = lax.psum(
        (
            positions_grad,
            merge_bias_grad,
            first_gain_grad,
            first_shift_grad,
            down_bias_grad,
            second_gain_grad,
            second_shift_grad,
        ),
        ("dp", "tensor"),
    )
    return (
        layer_out,
        tokens_grad,
        positions_grad,
        heads_weight_grad,
        merge_weight_grad,
        merge_bias_grad,
        first_gain_grad,
        first_shift_grad,
        up_weight_grad,
        up_bias_grad,
        down_weight_grad,
        down_bias_grad,
        second_gain_grad,
        second_shift_grad,
    )


def solution(mesh):
    in_specs = (
        P(("dp", "tensor"), None),
        P("dp", None),
        P(),
        P(None, None, "tensor"),
        P("tensor", None),
        P(),
        P(),
        P(),
        P(None, "tensor"),
        P("tensor"),
        P("tensor", None),
        P(),
        P(),
        P(),
        P(("dp", "tensor"), None),
    )
    out_specs = (
        P(("dp", "tensor"), None),
        P(("dp", "tensor"), None),
        P(),
        P(None, None, "tensor"),
        P("tensor", None),
        P(),
        P(),
        P(),
        P(None, "tensor"),
        P("tensor"),
        P("tensor", None),
        P(),
        P(),
        P(),
    )
    return jax.shard_map(
        per_device, mesh=mesh, in_specs=in_specs, out_specs=out_specs, check_vma=False
    )
```

profile of v0, /device:TPU:0, one launch (start us, length us, event | category | flops | bytes accessed | tf_op | source)
XLA Modules:
  0.0 790.6 jit_solution(13856556758043356244)
XLA Ops:
  11.3 35.9 %all-gather.5.cloned.1.call-done = bf16[2048,512]{1,0:T(8,128)(2,1)} async-done(((bf16[1024,512]{1,0:T(8,128)(2,1)}), bf16[2048,512]{1,0:T(8,128)(2,1)}) %all-gather.5.cloned.1.call-update) | async-done | bytes 2097168 | tf_op jit(solution)/shard_map/all_gather | solution.py:56
  47.2 5.1 convolution_convert_fusion
  52.3 4.7 copy.42
  57.0 6.1 reshape.228
  63.1 3.2 slice_bitcast_fusion
  68.2 20.5 %while.22 = (s32[]{:T(128)}, bf16[4,512,4,64]{1,3,2,0:T(8,128)(2,1)}, f32[4,4,512]{2,1,0:T(4,128)S(1)}, bf16[4,512,4,64]{1,3,2,0:T(8,128)(2,1)}, s32[4,512]{1,0:...) while((s32[]{:T(128)}, ...), condition=%wide.region_3.4_spmd, body=%wide.region_0.3_spmd.sunk | while | flops 281933824 | bytes 14753885 | solution.py:80
  70.3 3.0 fusion.152
  75.4 3.0 fusion.152
  80.5 3.0 fusion.152
  85.6 3.0 fusion.152
  88.7 2.8 copy.46
  92.8 2.7 fusion.100
  96.2 53.8 %reduce-scatter.5.cloned.1.call-done = f32[1024,512]{1,0:T(8,128)} async-done(((f32[2048,512]{1,0:T(8,128)}), f32[1024,512]{1,0:T(8,128)}) %reduce-scatter.5.cloned.1.call-update) | async-done | bytes 2097168 | tf_op jit(solution)/shard_map/reduce_scatter | solution.py:83
  149.9 2.6 fusion.99
  154.7 33.0 %all-gather.7.cloned.1.call-done = bf16[2048,512]{1,0:T(8,128)(2,1)} async-done(((bf16[1024,512]{1,0:T(8,128)(2,1)}), bf16[2048,512]{1,0:T(8,128)(2,1)}) %all-gather.7.cloned.1.call-update) | async-done | bytes 2097168 | tf_op jit(solution)/shard_map/all_gather | solution.py:93
  187.7 7.9 fusion.72
  196.3 53.8 %reduce-scatter.7.cloned.1.call-done = f32[1024,512]{1,0:T(8,128)} async-done(((f32[2048,512]{1,0:T(8,128)}), f32[1024,512]{1,0:T(8,128)}) %reduce-scatter.7.cloned.1.call-update) | async-done | bytes 2097168 | tf_op jit(solution)/shard_map/reduce_scatter | solution.py:99
  250.1 2.3 fusion.98
  254.6 2.0 fusion.97
  259.2 33.2 %all-gather.9.cloned.1.call-done = bf16[2048,512]{1,0:T(8,128)(2,1)} async-done(((bf16[1024,512]{1,0:T(8,128)(2,1)}), bf16[2048,512]{1,0:T(8,128)(2,1)}) %all-gather.9.cloned.1.call-update) | async-done | bytes 2097168 | tf_op jit(solution)/shard_map/all_gather | solution.py:112
  292.4 4.1 fusion.101
  296.5 7.2 convert_reduce_fusion
  303.8 2.0 copy-done.39
  305.7 4.3 fusion.102
  310.3 54.2 %reduce-scatter.9.cloned.1.call-done = f32[1024,512]{1,0:T(8,128)} async-done(((f32[2048,512]{1,0:T(8,128)}), f32[1024,512]{1,0:T(8,128)}) %reduce-scatter.9.cloned.1.call-update) | async-done | bytes 2097168 | tf_op jit(solution)/shard_map/reduce_scatter | solution.py:129
  364.5 2.8 multiply_reduce_fusion.1
  370.8 33.2 %all-gather.11.cloned.1.call-done = bf16[2048,512]{1,0:T(8,128)(2,1)} async-done(((bf16[1024,512]{1,0:T(8,128)(2,1)}), bf16[2048,512]{1,0:T(8,128)(2,1)}) %all-gather.11.cloned.1.call-update) | async-done | bytes 2097168 | tf_op jit(solution)/shard_map/all_gather | solution.py:137
  404.0 2.3 convolution_convert_fusion.1
  408.1 3.1 copy.50
  411.2 32.9 %while.23 = (s32[]{:T(128)}, bf16[4,512,3,4,64]{1,4,3,2,0:T(8,128)(2,1)}, bf16[4,512,4,64]{1,3,2,0:T(8,128)(2,1)S(1)}, s32[4,512]{1,0:T(4,128)S(1)}, bf16[4,512,...) while((s32[]{:T(128)}, ...), condition=%wide.region_17.18_spmd, body=%wide.region_15.17_spmd.sunk | while | flops 690616320 | bytes 36766320 | solution.py:175
  412.3 2.5 multiply_reduce_fusion.6
  420.5 2.5 multiply_reduce_fusion.6
  428.7 2.5 multiply_reduce_fusion.6
  436.9 2.5 multiply_reduce_fusion.6
  444.2 6.0 copy.52
  450.1 6.2 reshape.231
  456.4 5.1 bitcast_convert_fusion
  463.0 6.0 fusion.104
  469.0 8.5 %fusion.74 = f32[1024,512]{1,0:T(8,128)} fusion(bf16[2048,512]{1,0:T(8,128)(2,1)S(1)} %copy-done.34, f32[2048,1024]{1,0:T(8,128)} %copy-done.38, f32[1024]{0:T(1024)S(1)} %convert_element_type.111), kind=kOutput, calls=%fused_computation.89 | convolution fusion | flops 2168455168 | bytes 12587008 | tf_op jit(solution)/shard_map/rf,rd->fd/dot_general | solution.py:118
  479.6 3.0 fusion.79
  482.7 10.7 %reduce-scatter.11.cloned.1.call-done = bf16[1024,512]{1,0:T(8,128)(2,1)} async-done(((bf16[2048,512]{1,0:T(8,128)(2,1)}), bf16[1024,512]{1,0:T(8,128)(2,1)}) %reduce-scatter.11.cloned.1.call-update) | async-done | bytes 1048592 | tf_op jit(solution)/shard_map/reduce_scatter | solution.py:183
  496.3 1.9 copy-done.9
  498.3 3.7 reduce_sum.171
  502.0 35.5 %psum.91 = f32[1024]{0:T(1024)} all-reduce(f32[1024]{0:T(1024)S(1)} %get-tuple-element.193), channel_id=1, replica_groups=mesh['dp'=16,'tensor'=2] {'dp'}, use_global_device_ids=true, to_apply=%region_31.32 | all-reduce | flops 1024 | bytes 8192 | tf_op jit(solution)/shard_map/psum | solution.py:194
  537.6 37.5 %all-reduce = (f32[512]{0:T(512)}, f32[512]{0:T(512)}, f32[512]{0:T(512)}, f32[512]{0:T(512)}, f32[512]{0:T(512)}, /*index=5*/f32[512]{0:T(512)}) all-reduce(f32[512]{0:T(512)S(1)} %get-tuple-element.191, f32[512]{0:T(512)S(1)} %get-tuple-element.124, ...), channel_id=1, replica_groups=mesh['dp'=16,'tensor'=2] {'dp','tensor'}, use_global_device_ids=true, to_apply=%region_24.25 | all-reduce | flops 3072 | bytes 24576 | tf_op jit(solution)/shard_map/psum | solution.py:205
  575.0 63.6 %all-reduce.7.cloned.1.call-done = (f32[512,3,256]{2,0,1:T(8,128)}, f32[256,512]{1,0:T(8,128)}, f32[512,1024]{1,0:T(8,128)}, f32[1024,512]{1,0:T(8,128)}) async-done(((f32[512,3,256]{2,0,1:T(8,128)}, f32[256,512]{1,0:T(8,128)}, f32[512,1024]{1,0:T(8,128)}, f32[1024,512]{1,0:T(8,128)}), (f32[512,3,256]{2,0,1:T(8,128)}, f32[256,512]{1,0:T(8,128)}, f32[512,1024]{1,0:T(8,128)}, ...) | async-done | bytes 6291472 | tf_op jit(solution)/shard_map/psum | solution.py:194
  638.6 136.4 %all-reduce.5.cloned.1.call-done = f32[512,512]{1,0:T(8,128)} async-done(((f32[512,512]{1,0:T(8,128)}), f32[512,512]{1,0:T(8,128)}) %all-reduce.5.cloned.1.call-update) | async-done | bytes 1048592 | tf_op jit(solution)/shard_map/psum | solution.py:205
  775.0 2.3 copy.93
  (193 shorter events, 64.5 us)
Async XLA Ops:
  7.2 180.5 %copy-start = (bf16[512,1024]{1,0:T(8,128)(2,1)S(1)}, bf16[512,1024]{1,0:T(8,128)(2,1)}, u32[]{:S(2)}) copy-start(bf16[512,1024]{1,0:T(8,128)(2,1)} %param.27) | copy-start | bytes 3145732
  7.2 2.7 copy-start.13
  7.2 40.0 %all-gather.5.cloned.1.call-start = ((), (), s32[]{:S(2)}) async-start(), calls=%async_computation.4 | async-start | bytes 3145728 | tf_op jit(solution)/shard_map/all_gather | solution.py:56
  8.6 1.3 copy-start.10
  9.9 37.3 %copy-start.36 = (bf16[512,3,256]{2,0,1:T(8,128)(2,1)S(1)}, bf16[512,3,256]{2,0,1:T(8,128)(2,1)}, u32[]{:S(2)}) copy-start(bf16[512,3,256]{2,0,1:T(8,128)(2,1)} %param.22) | copy-start | bytes 2359300
  11.2 138.7 %reduce-scatter.5.cloned.1.call-start = ((), (), s32[]{:S(2)}) async-start(), calls=%async_computation.5 | async-start | bytes 6291456 | tf_op jit(solution)/shard_map/reduce_scatter | solution.py:83
  67.5 0.7 copy-start.23
  88.7 3.1 copy-start.2
  88.7 3.1 copy-start.4
  88.7 4.1 copy-start.21
  91.8 1.0 copy-start.11
  95.5 0.7 copy-start.26
  95.5 0.7 copy-start.27
  95.5 92.2 %all-gather.7.cloned.1.call-start = ((), (), s32[]{:S(2)}) async-start(), calls=%async_computation.6 | async-start | bytes 3145728 | tf_op jit(solution)/shard_map/all_gather | solution.py:93
  153.0 1.6 copy-start.24
  154.4 95.6 %reduce-scatter.7.cloned.1.call-start = ((), (), s32[]{:S(2)}) async-start(), calls=%async_computation.7 | async-start | bytes 6291456 | tf_op jit(solution)/shard_map/reduce_scatter | solution.py:99
  195.6 0.7 copy-start.29
  195.6 0.7 copy-start.30
  195.6 96.8 %all-gather.9.cloned.1.call-start = ((), (), s32[]{:S(2)}) async-start(), calls=%async_computation.8 | async-start | bytes 3145728 | tf_op jit(solution)/shard_map/all_gather | solution.py:112
  252.3 1.2 copy-start.14
  256.5 1.3 copy-start.8
  259.1 105.4 %reduce-scatter.9.cloned.1.call-start = ((), (), s32[]{:S(2)}) async-start(), calls=%async_computation.9 | async-start | bytes 6291456 | tf_op jit(solution)/shard_map/reduce_scatter | solution.py:129
  292.4 4.1 copy-start.33
  292.4 4.1 copy-start.35
  296.5 7.2 copy-start.38
  303.7 2.0 copy-start.39
  310.1 93.9 %all-gather.11.cloned.1.call-start = ((), (), s32[]{:S(2)}) async-start(), calls=%async_computation.10 | async-start | bytes 3145728 | tf_op jit(solution)/shard_map/all_gather | solution.py:137
  368.2 1.3 copy-start.6
  370.7 122.7 %reduce-scatter.11.cloned.1.call-start = ((), (), s32[]{:S(2)}) async-start(), calls=%async_computation.11 | async-start | bytes 3145728 | tf_op jit(solution)/shard_map/reduce_scatter | solution.py:183
  408.1 3.1 copy-start.3
  408.1 3.1 copy-start.5
  450.1 6.2 copy-start.37
  461.4 1.6 copy-start.32
  461.5 177.2 %all-reduce.7.cloned.1.call-start = ((), (), s32[]{:S(2)}) async-start(), calls=%async_computation.13 | async-start | bytes 12582912 | tf_op jit(solution)/shard_map/psum | solution.py:194
  463.0 6.0 copy-start.34
  469.0 8.5 %copy-start.12 = (bf16[32,8,4,512]{3,1,2,0:T(8,128)(2,1)S(1)}, bf16[32,8,4,512]{3,1,2,0:T(8,128)(2,1)}, u32[]{:S(2)}) copy-start(bf16[32,8,4,512]{3,1,2,0:T(8,128)(2,1)} %copy-done.11) | copy-start | bytes 3145732
  469.0 8.5 %copy-start.18 = (bf16[2048,512]{1,0:T(8,128)(2,1)S(1)}, bf16[2048,512]{1,0:T(8,128)(2,1)}, u32[]{:S(2)}) copy-start(bf16[2048,512]{1,0:T(8,128)(2,1)} %all-gather.11.cloned.1.call-done) | copy-start | bytes 6291460
  469.0 10.0 %copy-start.31 = (bf16[2048,512]{1,0:T(8,128)(2,1)S(1)}, bf16[2048,512]{1,0:T(8,128)(2,1)}, u32[]{:S(2)}) copy-start(bf16[2048,512]{1,0:T(8,128)(2,1)} %all-gather.5.cloned.1.call-done) | copy-start | bytes 6291460
  477.5 2.1 copy-start.15
  482.6 11.3 %copy-start.7 = (f32[1024,512]{1,0:T(8,128)S(1)}, f32[1024,512]{1,0:T(8,128)}, u32[]{:S(2)}) copy-start(f32[1024,512]{1,0:T(8,128)} %copy-done.6) | copy-start | bytes 6291460
  482.7 292.3 %all-reduce.5.cloned.1.call-start = ((), (), s32[]{:S(2)}) async-start(), calls=%async_computation.12 | async-start | bytes 2097152 | tf_op jit(solution)/shard_map/psum | solution.py:205
  493.5 1.2 copy-start.20
  496.3 1.9 copy-start.9
  638.6 138.6 %copy-start.19 = (f32[512,3,256]{2,0,1:T(8,128)S(1)}, f32[512,3,256]{2,0,1:T(8,128)}, u32[]{:S(2)}) copy-start(f32[512,3,256]{2,0,1:T(8,128)} %get-tuple-element.349) | copy-start | bytes 4718596
  777.3 1.4 copy-start.22
  777.3 2.3 copy-start.17
  779.6 2.3 copy-start.16
  779.6 3.7 copy-start.1
  (2 other events, 1.4 us)
Sparse Core Ops, SparseCore 0:
  11.3 35.8 all-gather.4
  95.6 54.2 reduce-scatter.4
  154.5 33.1 all-gather.6
  195.7 54.3 reduce-scatter.6
  259.2 33.1 all-gather.8
  310.2 54.2 reduce-scatter.8
  370.9 33.0 all-gather.10
  461.6 31.8 reduce-scatter.10
  498.0 140.6 all-reduce.6
  645.1 129.8 all-reduce.4
where the time goes:
time: 800 us; the launch traced here: 791 us
  waiting for transfers between devices  508 us (64%)
  matrix products  96.3 us (12%)
  blocking collectives  73 us (9%)
  local copies, waits for them, and re-layouts  59.7 us (7%)
  other arithmetic  37.2 us (5%)
  between operations  15 us (2%)
    psum x1, waiting for transfers between devices, per_device(): lax.psum((positions_grad, merge_bias_grad, first_gain_grad, first_shift_g...  136 us
    psum x1, waiting for transfers between devices, per_device(): lax.psum((heads_weight_grad, merge_weight_grad, up_weight_grad, up_bias_g...  63.6 us
    reduce_scatter x1, waiting for transfers between devices, per_device(): lax.psum_scatter(jnp.einsum('rf,df->rd', rows_part, up_weight, preferred_...  54.2 us
    reduce_scatter x1, waiting for transfers between devices, per_device(): lax.psum_scatter(jnp.dot(rows_part, down_weight, preferred_element_type=j...  53.8 us
    reduce_scatter x1, waiting for transfers between devices, per_device(): lax.psum_scatter(jnp.dot(rows_part, merge_weight, preferred_element_type=...  53.8 us
    psum x1, blocking collectives, per_device(): lax.psum((positions_grad, merge_bias_grad, first_gain_grad, first_shift_g...  37.5 us
    all_gather x1, waiting for transfers between devices, per_device(): lax.all_gather(start_sum.astype(jnp.bfloat16), 'tensor', axis=0, tiled=True)  35.9 us
    psum x1, blocking collectives, per_device(): lax.psum((heads_weight_grad, merge_weight_grad, up_weight_grad, up_bias_g...  35.5 us
  transfers between devices with their start and end apart: 10, of which 10 were waited for; matrix products, arithmetic and copies ran while one was open for 3% of the time, Pallas kernels for 0%

commit v1 on v0

v1 whole, which is shorter than its diff:
```python
import functools
import jax
import jax.numpy as jnp
from jax import lax
from jax.experimental import pallas as pl
from jax.experimental.pallas import tpu as pltpu
from jax.sharding import PartitionSpec as P

F32, BF16 = jnp.float32, jnp.bfloat16
HEAD = 64
ROWS = 256
NEG = -1000000000.0
GELU_A = 0.7978845608028654
GELU_B = GELU_A * 0.044715


def nn(a, b):
    return lax.dot_general(a, b, (((1,), (0,)), ((), ())), preferred_element_type=F32)


def nt(a, b):
    return lax.dot_general(a, b, (((1,), (1,)), ((), ())), preferred_element_type=F32)


def loop(count, body):
    lax.fori_loop(0, count, lambda i, c: (body(i), c)[1], 0)


def at(i, size):
    return pl.ds(pl.multiple_of(i * size, size), size)


def mean(v):
    return jnp.sum(v, -1, keepdims=True) * (1.0 / v.shape[-1])


def kernel(
    tok, seg, pos, cot, whp, wm, wu, wd, vec,
    out, tg, gd, gu, gm, gh, pg_out, vg,
    ai, ait, trip, bias, probs, mix, mixt, n1, r1, nb, nbt, hid, gp, gs, bg, bgt, mg, dtrip, acc,
):
    R, D = tok.shape
    T = pos.shape[0]
    W = R // T
    FH = wu.shape[2]
    C = 128
    tiles = R // ROWS
    per = T // ROWS
    lane = lax.broadcasted_iota(jnp.int32, (1, C), 1)
    t_id = lax.axis_index("tensor")

    def qkv(j):
        rows = at(j, ROWS)
        x = tok[rows, :].astype(F32) + pos[at(lax.rem(j, per), ROWS), :].astype(F32)
        xb = x.astype(BF16)
        ai[rows, :] = xb
        ait[:, rows] = xb.T

    loop(tiles, qkv)

    def qkv_half(h):
        def body(j):
            rows = at(j, ROWS)
            xb = ai[rows, :]
            for p in range(2):
                y = nn(xb, whp[h, p]).astype(BF16)
                trip[2 * h + p, rows, 0:C] = y[:, 0:C] * 0.125
                trip[2 * h + p, rows, C:] = y[:, C:]

        loop(tiles, body)

    for w in range(W):
        row = seg[pl.ds(t_id * W + w, 1), :].astype(F32)
        wide = jnp.broadcast_to(row, (128, T))
        col = wide.T
        for tb in range(per):
            nk = (tb + 1) * ROWS
            for c2 in range(ROWS // 128):
                lo = tb * ROWS + c2 * 128
                s_id = lax.broadcasted_iota(jnp.int32, (nk, 128), 0)
                l_id = lax.broadcasted_iota(jnp.int32, (nk, 128), 1) + lo
                ok = (col[:nk] == row[:, lo : lo + 128]) & (s_id <= l_id)
                bias[w, :nk, lo : lo + 128] = jnp.where(ok, 0.0, NEG)

    def attend(p, w):
        rows = at(w, T)
        cols = at(p, C)
        q = trip[p, rows, 0:C]
        k = trip[p, rows, C : 2 * C]
        vt = trip[p, rows, 2 * C :].T
        for tb in range(per):
            nk = (tb + 1) * ROWS
            ts = slice(tb * ROWS, (tb + 1) * ROWS)
            parts = []
            for a in range(2):
                qa = jnp.where((lane < HEAD) == (a == 0), q[ts], jnp.zeros((), BF16))
                s = nt(k[:nk], qa) + bias[w, :nk, ts]
                e = jnp.exp(s - jnp.max(s, 0, keepdims=True))
                pt = (e * (1.0 / jnp.sum(e, 0, keepdims=True))).astype(BF16)
                probs[w, 2 * p + a, :nk, ts] = pt
                parts.append(nn(vt[a * HEAD : (a + 1) * HEAD, :nk], pt))
            m = jnp.concatenate(parts, 0).astype(BF16)
            lanes = pl.ds(pl.multiple_of(w * T + tb * ROWS, ROWS), ROWS)
            mixt[cols, lanes] = m
            mix[lanes, cols] = m.T

    def attend_half(h):
        loop(2 * W, lambda i: attend(2 * h + i // W, lax.rem(i, W)))

    for h in range(2):
        qkv_half(h)
        attend_half(h)

    mb, g1, s1, db, g2, s2 = [vec[0, i : i + 1, :] for i in range(6)]
    acc[...] = jnp.zeros_like(acc)

    def rowsum(i, v):
        acc[pl.ds(8 * i, 8), :] += jnp.sum(v.reshape(-1, 8, v.shape[-1]), 0)

    def merge(j):
        rows = at(j, ROWS)
        x = tok[rows, :].astype(F32) + pos[at(lax.rem(j, per), ROWS), :].astype(F32)
        f = x + nn(mix[rows, :], wm[...]) + mb
        z = f - mean(f)
        r = lax.rsqrt(mean(z * z) + 1e-5)
        n = z * r
        n1[rows, :] = n
        r1[rows, :] = jnp.broadcast_to(r, (ROWS, 128))
        y = (n * g1 + s1).astype(BF16)
        nb[rows, :] = y
        nbt[:, rows] = y.T

    loop(tiles, merge)

    def up(h):
        def body(j):
            rows = at(j, ROWS)
            x = nb[rows, :]
            for c in range(FH // D):
                cs = slice(c * D, (c + 1) * D)
                v = nn(x, wu[h, :, cs]) + vec[h, 6 + c : 7 + c, :]
                v2 = v * v
                th = jnp.tanh(v * (GELU_A + GELU_B * v2))
                half = 0.5 + 0.5 * th
                hv = v * half
                hid[h, rows, cs] = hv.astype(BF16)
                gp[h, rows, cs] = (half + hv * (1.0 - th) * (GELU_A + 3.0 * GELU_B * v2)).astype(BF16)

        loop(tiles, body)

    up(0)
    up(1)

    def down(j):
        rows = at(j, ROWS)
        n = n1[rows, :] * g1 + s1
        f = n + (nn(hid[0, rows, :], wd[0]) + nn(hid[1, rows, :], wd[1])) + db
        z = f - mean(f)
        r = lax.rsqrt(mean(z * z) + 1e-5)
        n2 = z * r
        out[rows, :] = (n2 * g2 + s2).astype(BF16)
        g = cot[rows, :].astype(F32)
        e = g * g2
        d = r * (e - mean(e) - n2 * mean(e * n2))
        gs[rows, :] = d
        b = d.astype(BF16)
        bg[rows, :] = b
        bgt[:, rows] = b.T
        rowsum(0, g * n2)
        rowsum(1, g)
        rowsum(2, d)

    loop(tiles, down)

    for h in (1, 0):
        def body(c, h=h):
            gd[h, :, at(c, D)] = nn(bgt[...], hid[h, :, at(c, D)]).astype(BF16)

        loop(FH // D, body)

    def hidden_back(j):
        rows = at(j, ROWS)
        b = bg[rows, :]
        for h in range(2):
            for c in range(FH // D):
                cs = slice(c * D, (c + 1) * D)
                v = nt(b, wd[h, cs, :]) * gp[h, rows, cs].astype(F32)
                vb = v.astype(BF16)
                hid[h, rows, cs] = vb
                rowsum(3 + 2 * h + c, vb.astype(F32))

    loop(tiles, hidden_back)
    for h in (1, 0):
        def body(c, h=h):
            gu[h, :, at(c, D)] = nn(nbt[...], hid[h, :, at(c, D)]).astype(BF16)

        loop(FH // D, body)

    def first_back(j):
        rows = at(j, ROWS)
        g = gs[rows, :] + (nt(hid[0, rows, :], wu[0]) + nt(hid[1, rows, :], wu[1]))
        n = n1[rows, :]
        e = g * g1
        d = r1[rows, 0:1] * (e - mean(e) - n * mean(e * n))
        gs[rows, :] = d
        b = d.astype(BF16)
        bg[rows, :] = b
        mg[rows, :] = nt(b, wm[...]).astype(BF16)
        rowsum(7, g * n)
        rowsum(8, g)
        rowsum(9, d)

    loop(tiles, first_back)
    gm[...] = nn(mixt[...], bg[...]).astype(BF16)

    def attend_back(p, w):
        rows = at(w, T)
        cols = at(p, C)
        q = trip[p, rows, 0:C]
        k = trip[p, rows, C : 2 * C]
        v = trip[p, rows, 2 * C :]
        do = mg[rows, cols]
        kt = k.T
        prod = do.T.astype(F32) * mixt[cols, rows].astype(F32)
        dk, dv = None, None
        dq = []
        for tb in reversed(range(per)):
            nk = (tb + 1) * ROWS
            ts = slice(tb * ROWS, (tb + 1) * ROWS)
            pts, dss, qas, dos, dqs = [], [], [], [], []
            for a in range(2):
                mine = (lane < HEAD) == (a == 0)
                doa = jnp.where(mine, do[ts], jnp.zeros((), BF16))
                qa = jnp.where(mine, q[ts], jnp.zeros((), BF16))
                inner = jnp.sum(prod[a * HEAD : (a + 1) * HEAD, ts], 0, keepdims=True)
                pt = probs[w, 2 * p + a, :nk, ts]
                ds = (pt.astype(F32) * (nt(v[:nk], doa) - inner)).astype(BF16)
                dqs.append(nn(kt[a * HEAD : (a + 1) * HEAD, :nk], ds))
                pts.append(pt)
                dss.append(ds)
                qas.append(qa)
                dos.append(doa)
            dkb = nn(jnp.concatenate(dss, 1), jnp.concatenate(qas, 0))
            dvb = nn(jnp.concatenate(pts, 1), jnp.concatenate(dos, 0))
            if dk is None:
                dk, dv = dkb, dvb
            else:
                dk = jnp.concatenate([dk[:nk] + dkb, dk[nk:]], 0)
                dv = jnp.concatenate([dv[:nk] + dvb, dv[nk:]], 0)
            lanes = pl.ds(pl.multiple_of(w * T + tb * ROWS, ROWS), ROWS)
            dtrip[p, lanes, 0:C] = (jnp.concatenate(dqs, 0) * 0.125).astype(BF16).T
        dtrip[p, rows, C : 2 * C] = dk.astype(BF16)
        dtrip[p, rows, 2 * C :] = dv.astype(BF16)

    for i in range(2):
        for h in (1, 0):
            loop(W, lambda w: attend_back(2 * h + i, w))
            gh[h, i] = nn(ait[...], dtrip[2 * h + i]).astype(BF16)

    def last(j):
        total = jnp.zeros((ROWS, D), F32)
        for w in range(W):
            rows = pl.ds(pl.multiple_of(w * T + j * ROWS, ROWS), ROWS)
            g = gs[rows, :]
            for p in range(4):
                g += nt(dtrip[p, rows, :], whp[p // 2, p % 2])
            tg[rows, :] = g
            total += g
        pg_out[at(j, ROWS), :] = total.astype(BF16)

    loop(per, last)
    for i in range(10):
        vg[i : i + 1, :] = jnp.sum(acc[8 * i : 8 * i + 8, :], 0, keepdims=True)


def scratch(R, D, T, FH):
    W = R // T
    V = pltpu.VMEM
    return [
        V((R, D), BF16), V((D, R), BF16), V((4, R, 384), BF16), V((W, T, T), F32), V((W, 8, T, T), BF16),
        V((R, D), BF16), V((D, R), BF16), V((R, D), F32), V((R, 128), F32), V((R, D), BF16), V((D, R), BF16),
        V((2, R, FH), BF16), V((2, R, FH), BF16), V((R, D), F32), V((R, D), BF16), V((D, R), BF16),
        V((R, D), BF16), V((4, R, 384), BF16), V((80, D), F32),
    ]


def call(tok, seg, pos, cot, whp, wm, wu, wd, vec):
    R, D = tok.shape
    T = pos.shape[0]
    FH = wu.shape[2]
    S = jax.ShapeDtypeStruct
    vm = pl.BlockSpec(memory_space=pltpu.VMEM)
    outs = [
        S((R, D), BF16), S((R, D), F32), S((2, D, FH), BF16), S((2, D, FH), BF16), S((D, D), BF16),
        S((2, 2, D, 384), BF16), S((T, D), BF16), S((16, D), F32),
    ]
    return pl.pallas_call(
        kernel,
        out_shape=outs,
        in_specs=[vm] * 9,
        out_specs=[vm] * len(outs),
        scratch_shapes=scratch(R, D, T, FH),
        compiler_params=pltpu.CompilerParams(vmem_limit_bytes=63 * 2**20),
    )(tok, seg, pos, cot, whp, wm, wu, wd, vec)


def per_device(tok, seg, pos, hw, mw, mb, g1, s1, uw, ub, dw, db, g2, s2, cot):
    D = tok.shape[1]
    half = hw.shape[2]
    whp = hw.reshape(D, 3, 2, 128).transpose(2, 0, 1, 3).reshape(2, D, 384)
    vec = jnp.concatenate([v.astype(F32) for v in (mb, g1, s1, db, g2, s2, ub)]).reshape(8, D)
    swap = lambda v: jnp.stack([v, lax.ppermute(v, "tensor", [(0, 1), (1, 0)])])
    whp, wm, wu, wd, vec = swap(whp), swap(mw).reshape(2 * half, D), swap(uw), swap(dw), swap(vec)
    out, tg, gd, gu, gm, gh, pg, vg = call(tok, seg, pos, cot, whp, wm, wu, wd, vec)
    gm = gm.reshape(2, half, D)
    pick = lambda v: lax.psum(v[0] + lax.ppermute(v[1], "tensor", [(0, 1), (1, 0)]), "dp").astype(F32)
    gd, gu, gm, gh = pick(gd), pick(gu), pick(gm), pick(gh)
    vg_own = lax.psum(vg, "dp")
    rest = lax.psum(vg, ("dp", "tensor"))
    ubg = lax.psum(vg[3:5] + lax.ppermute(vg[5:7], "tensor", [(0, 1), (1, 0)]), "dp").reshape(-1)
    pg = lax.psum(pg.astype(F32), ("dp", "tensor"))
    hg = gh.reshape(2, D, 3, 128).transpose(1, 2, 0, 3).reshape(D, 3, half)
    return (out, tg, pg, hg, gm, rest[9], rest[7], rest[8], gu, ubg, gd.T, rest[2], rest[0], rest[1])


def solution(mesh):
    rows = P(("dp", "tensor"), None)
    ins = (rows, P("dp", None), P(), P(None, None, "tensor"), P("tensor", None), P(), P(), P(), P(None, "tensor"), P("tensor"),
           P("tensor", None), P(), P(), P(), rows)
    outs = (rows, rows, P(), P(None, None, "tensor"), P("tensor", None), P(), P(), P(), P(None, "tensor"), P("tensor"),
            P("tensor", None), P(), P(), P())
    return jax.shard_map(per_device, mesh=mesh, in_specs=ins, out_specs=outs, check_vma=False)
```

time: 800 us -> 359 us (0.45); the launches traced: 791 us -> 358 us
  waiting for transfers between devices: 508 us -> 137 us
  matrix products: 96.3 us -> 0 us
  Pallas kernels: 0 us -> 71.3 us
  local copies, waits for them, and re-layouts: 59.7 us -> 15 us
  other arithmetic: 37.2 us -> 19.4 us
  blocking collectives: 73 us -> 88.6 us
  starting transfers between devices: 1.05 us -> 12.9 us
    psum x2 -> x1, waiting for transfers between devices: 200 us -> 15.8 us  [per_device(): lax.psum(v[0] + lax.ppermute(v[1], 'tensor', [(0, 1), (1, 0)]), 'dp')]
    reduce_scatter x4 -> x0, waiting for transfers between devices: 172 us -> none  [the longest x1 54.2 us: per_device(): lax.psum_scatter(jnp.einsum('rf,df->rd', rows_part, up_weight, preferred_...]
    all_gather x4 -> x0, waiting for transfers between devices: 135 us -> none  [the longest x1 35.9 us: per_device(): lax.all_gather(start_sum.astype(jnp.bfloat16), 'tensor', axis=0, tiled=True)]
    ppermute x0 -> x10, waiting for transfers between devices: none -> 121 us  [the longest x5 60.9 us: per_device(): swap = lambda v: jnp.stack([v, lax.ppermute(v, 'tensor', [(0, 1), (1, 0)])])]
    dot_general x40 -> x0, matrix products: 96.3 us -> none  [the longest x4 12.2 us: attend(): jnp.einsum('hts,shd->thd', probs.astype(jnp.bfloat16), win_values, prefer...]
    pallas_call x0 -> x1, Pallas kernels: none -> 71.3 us  [call(): pl.pallas_call(kernel, out_shape=outs, in_specs=[vm] * 9, out_specs=[vm]...]
    reduce_sum x15 -> x0, other arithmetic: 22.1 us -> none  [the longest x2 4.93 us: layer_norm(): center = jnp.mean(value, -1, keepdims=True)]
    psum x2, blocking collectives: 73 us -> 88.6 us  [the longest x1 56.8 us: per_device(): pg = lax.psum(pg.astype(F32), ('dp', 'tensor'))]
  transfers between devices with their start and end apart: 10 -> 11, of which waited for: 10 -> 5; matrix products, arithmetic and copies ran while one was open for 3% -> 5% of each run, Pallas kernels for 0% -> 0%
where the time goes in v1:
time: 359 us; the launch traced here: 358 us
  waiting for transfers between devices  137 us (38%)
  blocking collectives  88.6 us (25%)
  Pallas kernels  71.3 us (20%)
  other arithmetic  19.4 us (5%)
  local copies, waits for them, and re-layouts  15 us (4%)
  between operations  14.2 us (4%)
  starting transfers between devices  12.9 us (4%)
    pallas_call x1, Pallas kernels, call(): pl.pallas_call(kernel, out_shape=outs, in_specs=[vm] * 9, out_specs=[vm]...  71.3 us
    ppermute x5, waiting for transfers between devices, per_device(): swap = lambda v: jnp.stack([v, lax.ppermute(v, 'tensor', [(0, 1), (1, 0)])])  60.9 us
    ppermute x4, waiting for transfers between devices, per_device(): lax.ppermute(v[1], 'tensor', [(0, 1), (1, 0)])  57.7 us
    psum x1, blocking collectives, per_device(): pg = lax.psum(pg.astype(F32), ('dp', 'tensor'))  56.8 us
    psum x1, blocking collectives, per_device(): lax.psum(vg[3:5] + lax.ppermute(vg[5:7], 'tensor', [(0, 1), (1, 0)]), 'dp')  31.7 us
    psum x1, waiting for transfers between devices, per_device(): lax.psum(v[0] + lax.ppermute(v[1], 'tensor', [(0, 1), (1, 0)]), 'dp')  15.8 us
    another operation x5, other arithmetic, per_device(): swap = lambda v: jnp.stack([v, lax.ppermute(v, 'tensor', [(0, 1), (1, 0)])])  10.5 us
    unnamed x44, local copies, waits for them, and re-layouts  7.64 us
  transfers between devices with their start and end apart: 11, of which 5 were waited for; matrix products, arithmetic and copies ran while one was open for 5% of the time, Pallas kernels for 0%

profile of v1, /device:TPU:0, one launch (start us, length us, event | category | flops | bytes accessed | tf_op | source)
XLA Modules:
  0.0 358.0 jit_solution(4607564185751402736)
XLA Ops:
  7.3 3.0 collective-permute-start.2
  10.3 1.4 copy.36
  11.8 0.1 copy.37
  11.8 0.4 copy.39
  12.2 0.2 collective-permute-start
  12.4 1.9 collective-permute-start.3
  14.3 0.1 collective-permute-start.1
  14.4 0.2 dynamic-update-slice
  14.6 0.2 dynamic-update-slice.1
  14.8 0.2 dynamic-update-slice.2
  15.0 0.2 dynamic-update-slice.3
  15.3 0.2 dynamic-update-slice.4
  15.5 0.2 dynamic-update-slice.5
  15.7 2.0 collective-permute-start.4
  17.7 0.4 copy.40
  18.1 60.9 %collective-permute-done.4 = f32[8,512]{1,0:T(8,128)S(1)} collective-permute-done((f32[8,512]{1,0:T(8,128)S(1)}, f32[8,512]{1,0:T(8,128)S(1)}, u32[]{:S(2)}, u32[]{:S(2)}) %collective-permute-start.4) | collective-permute-done | bytes 16416 | tf_op jit(solution)/shard_map/ppermute | solution.py:312
  79.0 0.6 pad_maximum_fusion.4.vec
  79.6 2.0 pad_maximum_fusion.3
  81.6 2.5 pad_maximum_fusion.2.whp
  84.1 2.7 pad_maximum_fusion.wu
  86.8 2.7 pad_maximum_fusion.1.wd
  89.5 71.3 %shard_map.254 = (bf16[1024,512]{1,0:T(8,128)(2,1)}, f32[1024,512]{1,0:T(8,128)}, bf16[2,512,1024]{2,1,0:T(8,128)(2,1)}, bf16[2,512,1024]{2,1,0:T(8,128)(2,1)}, ...) custom-call(bf16[1024,512]{1,0:T(8,128)(2,1)} %tok.1, ...), custom_call_target="tpu_custom_call" | custom-call | tf_op jit(solution)/shard_map/pallas_call | solution.py:297
  160.9 1.4 slice_bitcast_fusion.2
  162.2 1.8 collective-permute-start.5
  164.0 2.3 slice_bitcast_fusion
  166.3 0.3 collective-permute-start.9
  166.6 1.8 collective-permute-start.6
  168.4 1.0 slice_bitcast_fusion.1
  169.5 0.3 collective-permute-start.7
  169.7 41.1 %collective-permute-done.6 = bf16[256,512]{1,0:T(8,128)(2,1)S(1)} collective-permute-done((bf16[256,512]{1,0:T(8,128)(2,1)S(1)}, bf16[256,512]{1,0:T(8,128)(2,1)S(1)}, u32[]{:S(2)}, u32[]{:S(2)}) %collective-permute-start.6) | collective-permute-done | bytes 262176 | tf_op jit(solution)/shard_map/ppermute | solution.py:316
  210.9 0.7 slice_add_fusion
  211.6 0.1 bitcast_add_fusion.2
  211.7 0.3 copy.41
  212.0 0.9 copy.42
  212.9 2.3 fusion
  215.2 16.6 %collective-permute-done.7 = bf16[512,1024]{1,0:T(8,128)(2,1)} collective-permute-done((bf16[512,1024]{1,0:T(8,128)(2,1)}, bf16[512,1024]{1,0:T(8,128)(2,1)}, u32[]{:S(2)}, u32[]{:S(2)}) %collective-permute-start.7) | collective-permute-done | bytes 1048608 | tf_op jit(solution)/shard_map/ppermute | solution.py:316
  231.8 2.3 bitcast_add_fusion.1
  234.2 0.7 copy-done.9
  234.9 1.4 collective-permute-start.8
  236.3 2.2 collective-permute-done.8
  238.5 31.7 %psum.54 = f32[1024]{0:T(1024)} all-reduce(f32[1024]{0:T(1024)S(1)} %bitcast.51), channel_id=1, replica_groups=mesh['dp'=16,'tensor'=2] {'dp'}, use_global_device_ids=true, to_apply=%region_5.0 | all-reduce | flops 1024 | bytes 8192 | tf_op jit(solution)/shard_map/psum | solution.py:320
  270.3 56.8 %all-reduce.6 = (f32[512,512]{1,0:T(8,128)}, f32[16,512]{1,0:T(8,128)S(1)}) all-reduce(bf16[512,512]{1,0:T(8,128)(2,1)S(1)} %copy-done.8, f32[16,512]{1,0:T(8,128)S(1)} %copy-done.9), channel_id=1, replica_groups=mesh['dp'=16,'tensor'=2] {'dp','tensor'}, use_global_device_ids=true, to_apply=%region_0.0 | all-reduce | flops 270336 | bytes 1638400 | tf_op jit(solution)/shard_map/psum | solution.py:321
  327.1 0.6 fusion.1
  327.7 15.8 %all-reduce.5.cloned.1.call-done = (bf16[512,3,256]{0,2,1:T(8,128)(2,1)}, bf16[1024,512]{0,1:T(8,128)(2,1)}, bf16[256,512]{1,0:T(8,128)(2,1)}, bf16[512,1024]{1,0:T(8,128)(2,1)}) async-done(((bf16[512,3,256]{0,2,1:T(8,128)(2,1)}, bf16[1024,512]{0,1:T(8,128)(2,1)}, bf16[256,512]{1,0:T(8,128)(2,1)}, bf16[512,1024]{1,0:T(8,128)(2,1)}), (bf16[512,3,256]{0,2,1:T(8,128)(2,1)}, bf16[1024,512]{0,1:T(8,128)(2,1)}, ...) | async-done | bytes 3145744 | tf_op jit(solution)/shard_map/psum | solution.py:316
  343.6 1.9 convert_element_type.7
  345.4 2.5 copy.43
  348.0 1.6 copy.44
  349.6 1.6 convert_element_type.8
  (49 shorter events, 0.2 us)
Async XLA Ops:
  7.2 5.2 %copy-start.6 = (bf16[1024,512]{1,0:T(8,128)(2,1)S(1)}, bf16[1024,512]{1,0:T(8,128)(2,1)}, u32[]{:S(2)}) copy-start(bf16[1024,512]{1,0:T(8,128)(2,1)} %param.25) | copy-start | bytes 3145732
  7.2 7.2 %copy-start.11 = (bf16[512]{0:T(512)(128)(2,1)S(1)}, bf16[512]{0:T(512)(128)(2,1)}, u32[]{:S(2)}) copy-start(bf16[512]{0:T(512)(128)(2,1)} %param.20) | copy-start | bytes 3076
  7.2 7.4 %copy-start.12 = (bf16[512]{0:T(512)(128)(2,1)S(1)}, bf16[512]{0:T(512)(128)(2,1)}, u32[]{:S(2)}) copy-start(bf16[512]{0:T(512)(128)(2,1)} %param.21) | copy-start | bytes 3076
  7.2 7.6 %copy-start.13 = (bf16[512]{0:T(512)(128)(2,1)S(1)}, bf16[512]{0:T(512)(128)(2,1)}, u32[]{:S(2)}) copy-start(bf16[512]{0:T(512)(128)(2,1)} %param.22) | copy-start | bytes 3076
  7.2 7.8 %copy-start.14 = (bf16[512]{0:T(512)(128)(2,1)S(1)}, bf16[512]{0:T(512)(128)(2,1)}, u32[]{:S(2)}) copy-start(bf16[512]{0:T(512)(128)(2,1)} %param.26) | copy-start | bytes 3076
  7.2 8.0 %copy-start.15 = (bf16[512]{0:T(512)(128)(2,1)S(1)}, bf16[512]{0:T(512)(128)(2,1)}, u32[]{:S(2)}) copy-start(bf16[512]{0:T(512)(128)(2,1)} %param.27) | copy-start | bytes 3076
  7.2 8.2 %copy-start.16 = (bf16[512]{0:T(512)(128)(2,1)S(1)}, bf16[512]{0:T(512)(128)(2,1)}, u32[]{:S(2)}) copy-start(bf16[512]{0:T(512)(128)(2,1)} %param.28) | copy-start | bytes 3076
  7.3 8.5 %copy-start.10 = (bf16[1024]{0:T(1024)(128)(2,1)S(1)}, bf16[1024]{0:T(1024)(128)(2,1)}, u32[]{:S(2)}) copy-start(bf16[1024]{0:T(1024)(128)(2,1)} %param.24) | copy-start | bytes 6148
  7.3 336.3 %all-reduce.5.cloned.1.call-start = ((), (), s32[]{:S(2)}) async-start(), calls=%async_computation | async-start | bytes 6291456 | tf_op jit(solution)/shard_map/psum | solution.py:316
  7.3 76.7 %collective-permute-start.2 = (bf16[512,1024]{1,0:T(8,128)(2,1)}, bf16[512,1024]{1,0:T(8,128)(2,1)}, u32[]{:S(2)}, u32[]{:S(2)}) collective-permute-start(bf16[512,1024]{1,0:T(8,128)(2,1)} %param.23), channel_id=1, source_target_pairs={{0,1},{1,0},{2,3},{3,2},{4,5},{5,4},{6,7},{7,6},{8,9},{9,8},{10,11... | collective-permute-start | bytes 3145736 | tf_op jit(solution)/shard_map/ppermute | solution.py:312
  12.2 69.4 %collective-permute-start = (bf16[2,512,384]{2,1,0:T(8,128)(2,1)S(1)}, bf16[2,512,384]{2,1,0:T(8,128)(2,1)}, u32[]{:S(2)}, u32[]{:S(2)}) collective-permute-start(bf16[2,512,384]{2,1,0:T(8,128)(2,1)S(1)} %copy.39), channel_id=1, source_target_pairs={{0,1},{1,0},{2,3},{3,2},{4,5},{5,4},{6,7},{7,6},{8,9},{9,8},{10,11... | collective-permute-start | bytes 2359304 | tf_op jit(solution)/shard_map/ppermute | solution.py:312
  12.4 74.4 %collective-permute-start.3 = (bf16[1024,512]{1,0:T(8,128)(2,1)S(1)}, bf16[1024,512]{1,0:T(8,128)(2,1)}, u32[]{:S(2)}, u32[]{:S(2)}) collective-permute-start(bf16[1024,512]{1,0:T(8,128)(2,1)S(1)} %copy-done.6), channel_id=1, source_target_pairs={{0,1},{1,0},{2,3},{3,2},{4,5},{5,4},{6,7},{7,6},{8,9},{9,8},{10,11... | collective-permute-start | bytes 3145736 | tf_op jit(solution)/shard_map/ppermute | solution.py:312
  14.3 65.3 %collective-permute-start.1 = (bf16[256,512]{1,0:T(8,128)(2,1)}, bf16[256,512]{1,0:T(8,128)(2,1)}, u32[]{:S(2)}, u32[]{:S(2)}) collective-permute-start(bf16[256,512]{1,0:T(8,128)(2,1)} %param.19), channel_id=1, source_target_pairs={{0,1},{1,0},{2,3},{3,2},{4,5},{5,4},{6,7},{7,6},{8,9},{9,8},{10,11... | collective-permute-start | bytes 786440 | tf_op jit(solution)/shard_map/ppermute | solution.py:312
  15.7 63.3 %collective-permute-start.4 = (f32[8,512]{1,0:T(8,128)S(1)}, f32[8,512]{1,0:T(8,128)S(1)}, u32[]{:S(2)}, u32[]{:S(2)}) collective-permute-start(f32[8,512]{1,0:T(8,128)S(1)} %reshape.61), channel_id=1, source_target_pairs={{0,1},{1,0},{2,3},{3,2},{4,5},{5,4},{6,7},{7,6},{8,9},{9,8},{10,11... | collective-permute-start | bytes 49160 | tf_op jit(solution)/shard_map/ppermute | solution.py:312
  79.6 4.4 %copy-start.5 = (bf16[512,1024]{1,0:T(8,128)(2,1)S(1)}, bf16[512,1024]{1,0:T(8,128)(2,1)}, u32[]{:S(2)}) copy-start(bf16[512,1024]{1,0:T(8,128)(2,1)} %param.23) | copy-start | bytes 3145732
  160.9 5.7 %copy-start.7 = (bf16[512,512]{1,0:T(8,128)(2,1)S(1)}, bf16[512,512]{1,0:T(8,128)(2,1)}, u32[]{:S(2)}) copy-start(bf16[512,512]{1,0:T(8,128)(2,1)} %get-tuple-element.26) | copy-start | bytes 1572868
  160.9 7.6 %copy-start = (bf16[2,512,1024]{2,1,0:T(8,128)(2,1)S(1)}, bf16[2,512,1024]{2,1,0:T(8,128)(2,1)}, u32[]{:S(2)}) copy-start(bf16[2,512,1024]{2,1,0:T(8,128)(2,1)} %get-tuple-element.28) | copy-start | bytes 6291460
  162.2 49.4 %collective-permute-start.5 = (bf16[2,512,384]{2,1,0:T(8,128)(2,1)S(1)}, bf16[2,512,384]{2,1,0:T(8,128)(2,1)S(1)}, u32[]{:S(2)}, u32[]{:S(2)}) collective-permute-start(bf16[2,512,384]{2,1,0:T(8,128)(2,1)S(1)} %slice_bitcast_fusion.2), channel_id=1, source_target_pairs={{0,1},{1,0},{2,3},{3,2},{4,5},{5,4},{6,7},{7,6},{8,9},{9,8},{10,11... | collective-permute-start | bytes 2359304 | tf_op jit(solution)/shard_map/ppermute | solution.py:316
  166.3 45.3 %copy-start.2 = (bf16[2,2,512,384]{3,2,1,0:T(8,128)(2,1)S(1)}, bf16[2,2,512,384]{3,2,1,0:T(8,128)(2,1)}, u32[]{:S(2)}) copy-start(bf16[2,2,512,384]{3,2,1,0:T(8,128)(2,1)} %get-tuple-element.25) | copy-start | bytes 4718596
  166.3 46.6 %collective-permute-start.9 = (bf16[512,1024]{1,0:T(8,128)(2,1)}, bf16[512,1024]{1,0:T(8,128)(2,1)S(1)}, u32[]{:S(2)}, u32[]{:S(2)}) collective-permute-start(bf16[512,1024]{1,0:T(8,128)(2,1)} %slice_bitcast_fusion), channel_id=1, source_target_pairs={{0,1},{1,0},{2,3},{3,2},{4,5},{5,4},{6,7},{7,6},{8,9},{9,8},{10,11... | collective-permute-start | bytes 3145736 | tf_op jit(solution)/shard_map/ppermute | solution.py:316
  166.6 44.3 %collective-permute-start.6 = (bf16[256,512]{1,0:T(8,128)(2,1)S(1)}, bf16[256,512]{1,0:T(8,128)(2,1)S(1)}, u32[]{:S(2)}, u32[]{:S(2)}) collective-permute-start(bf16[256,512]{1,0:T(8,128)(2,1)S(1)} %slice.53), channel_id=1, source_target_pairs={{0,1},{1,0},{2,3},{3,2},{4,5},{5,4},{6,7},{7,6},{8,9},{9,8},{10,11... | collective-permute-start | bytes 786440 | tf_op jit(solution)/shard_map/ppermute | solution.py:316
  169.5 62.3 %collective-permute-start.7 = (bf16[512,1024]{1,0:T(8,128)(2,1)}, bf16[512,1024]{1,0:T(8,128)(2,1)}, u32[]{:S(2)}, u32[]{:S(2)}) collective-permute-start(bf16[512,1024]{1,0:T(8,128)(2,1)} %slice_bitcast_fusion.1), channel_id=1, source_target_pairs={{0,1},{1,0},{2,3},{3,2},{4,5},{5,4},{6,7},{7,6},{8,9},{9,8},{10,11... | collective-permute-start | bytes 3145736 | tf_op jit(solution)/shard_map/ppermute | solution.py:316
  212.0 19.8 %copy-start.1 = (bf16[2,512,1024]{2,1,0:T(8,128)(2,1)S(1)}, bf16[2,512,1024]{2,1,0:T(8,128)(2,1)}, u32[]{:S(2)}) copy-start(bf16[2,512,1024]{2,1,0:T(8,128)(2,1)} %get-tuple-element.28) | copy-start | bytes 6291460
  234.1 0.8 copy-start.9
  234.1 36.1 %copy-start.8 = (bf16[512,512]{1,0:T(8,128)(2,1)S(1)}, bf16[512,512]{1,0:T(8,128)(2,1)}, u32[]{:S(2)}) copy-start(bf16[512,512]{1,0:T(8,128)(2,1)} %get-tuple-element.24) | copy-start | bytes 1572868
  234.9 3.6 %collective-permute-start.8 = (f32[2,512]{1,0:T(2,128)S(1)}, f32[2,512]{1,0:T(2,128)S(1)}, u32[]{:S(2)}, u32[]{:S(2)}) collective-permute-start(f32[2,512]{1,0:T(2,128)S(1)} %slice.60), channel_id=1, source_target_pairs={{0,1},{1,0},{2,3},{3,2},{4,5},{5,4},{6,7},{7,6},{8,9},{9,8},{10,11... | collective-permute-start | bytes 12296 | tf_op jit(solution)/shard_map/ppermute | solution.py:320
  343.5 4.4 %copy-start.4 = (bf16[1024,512]{0,1:T(8,128)(2,1)S(1)}, bf16[1024,512]{0,1:T(8,128)(2,1)}, u32[]{:S(2)}) copy-start(bf16[1024,512]{0,1:T(8,128)(2,1)} %get-tuple-element.75) | copy-start | bytes 3145732
  348.0 1.6 copy-start.3
Sparse Core Ops, SparseCore 0:
  234.3 109.2 all-reduce.4

commit v2 on v1

--- a/solution.py
+++ b/solution.py
@@ -7,6 +7,8 @@
 from jax.sharding import PartitionSpec as P
 
 F32, BF16 = jnp.float32, jnp.bfloat16
+MESH = pl.DeviceIdType.MESH
+VMEM_LIMIT = 64 * 2**20 - 2**18
 HEAD = 64
 ROWS = 256
 NEG = -1000000000.0
@@ -34,10 +36,187 @@
     return jnp.sum(v, -1, keepdims=True) * (1.0 / v.shape[-1])
 
 
+class Net:
+    def __init__(self, send_sem, recv_sem, dp):
+        self.send_sem, self.recv_sem, self.sent, self.count = send_sem, recv_sem, [], 0
+        i = lax.axis_index("dp")
+        self.t = lax.axis_index("tensor")
+        self.c = lax.rem(i, 2)
+        self.x = lax.rem(i // 2, 2)
+        self.z = lax.rem(i // 4, 4)
+        self.core = {"dp": i + 1 - 2 * self.c}
+        self.xdev = {"dp": i + 2 - 4 * self.x}
+        self.ydev = {"tensor": 1 - self.t}
+        self.zto = [lax.rem(self.z + s, 4) for s in range(1, 4)]
+        self.zdev = [{"dp": i + 4 * (j - self.z)} for j in self.zto]
+        self.extra = []
+        step = 16
+        while step < dp:
+            bit = lax.rem(i // step, 2)
+            self.extra.append({"dp": i + step * (1 - 2 * bit)})
+            step *= 2
+
+    def everyone(self):
+        return [self.core, self.xdev, self.ydev] + self.zdev + self.extra
+
+    def greet(self):
+        barrier = pltpu.get_barrier_semaphore()
+        for device in self.everyone():
+            pl.semaphore_signal(barrier, inc=1, device_id=device, device_id_type=MESH)
+        pl.semaphore_wait(barrier, len(self.everyone()))
+
+    def send(self, src, dst, device):
+        k = self.count
+        self.count += 1
+        copy = pltpu.make_async_remote_copy(
+            src_ref=src, dst_ref=dst, send_sem=self.send_sem.at[k], recv_sem=self.recv_sem.at[k],
+            device_id=device, device_id_type=MESH,
+        )
+        copy.start()
+        self.sent.append(copy)
+        return copy
+
+    def finish(self):
+        for copy in self.sent:
+            copy.wait_send()
+
+
+def tri(tb):
+    return slice(tb * (tb + 1) // 2 * ROWS, (tb + 1) * (tb + 2) // 2 * ROWS)
+
+
+def part(base, size):
+    return pl.ds(pl.multiple_of(base, size), size)
+
+
+def fetch_direct(net, own, oth):
+    half = own.shape[0] // 2
+    r = part(net.c * half, half)
+    y = net.send(own.at[r], oth.at[r], net.ydev)
+    yield
+    y.wait_recv()
+    c = net.send(oth.at[r], oth.at[r], net.core)
+    yield
+    c.wait_recv()
+    yield
+
+
+def fetch_shared(net, own, oth):
+    q = own.shape[0] // 4
+    a = part((2 * net.c + net.x) * q, q)
+    b = part((2 * net.c + 1 - net.x) * q, q)
+    y = net.send(own.at[a], oth.at[a], net.ydev)
+    yield
+    y.wait_recv()
+    x = net.send(oth.at[a], oth.at[a], net.xdev)
+    c0 = net.send(oth.at[a], oth.at[a], net.core)
+    yield
+    x.wait_recv()
+    c1 = net.send(oth.at[b], oth.at[b], net.core)
+    yield
+    c0.wait_recv()
+    c1.wait_recv()
+    yield
+
+
+def add(ref, at_rows, others, to=None):
+    total = ref[at_rows, :].astype(F32)
+    for other in others:
+        total = total + other.astype(F32)
+    (ref if to is None else to)[at_rows, :] = total.astype(BF16)
+
+
+def reduce(net, own, oth, rc, yr, xr, zr, er, fin, fin_oth=None):
+    rows = own.shape[0]
+    hr, qr, sr = rows // 2, rows // 4, rows // 16
+    mine = part(net.c * hr, hr)
+    c1 = net.send(oth.at[part((1 - net.c) * hr, hr)], rc.at[1], net.core)
+    c0 = net.send(own.at[part((1 - net.c) * hr, hr)], rc.at[0], net.core)
+    yield
+    c1.wait_recv()
+    add(oth, mine, [rc[1]])
+    y = net.send(oth.at[mine], yr, net.ydev)
+    yield
+    c0.wait_recv()
+    y.wait_recv()
+    add(own, mine, [rc[0], yr[...]])
+    x = net.send(own.at[part(net.c * hr + (1 - net.x) * qr, qr)], xr, net.xdev)
+    yield
+    x.wait_recv()
+    base = net.c * hr + net.x * qr
+    add(own, part(base, qr), [xr[...]])
+    zs = [net.send(own.at[part(base + j * sr, sr)], zr.at[s], net.zdev[s]) for s, j in enumerate(net.zto)]
+    yield
+    for z in zs:
+        z.wait_recv()
+    shard = part(base + net.z * sr, sr)
+    add(own, shard, [zr[0], zr[1], zr[2]], fin)
+    for b, device in enumerate(net.extra):
+        e = net.send(fin.at[shard], er.at[b], device)
+        yield
+        e.wait_recv()
+        e.wait_send()
+        net.sent = [o for o in net.sent if o is not e]
+        add(fin, shard, [er[b]])
+    zs = [net.send(fin.at[shard], fin.at[shard], device) for device in net.zdev]
+    yield
+    for z in zs:
+        z.wait_recv()
+    quarter = part(base, qr)
+    x = net.send(fin.at[quarter], fin.at[quarter], net.xdev)
+    yield
+    x.wait_recv()
+    c = net.send(fin.at[mine], fin.at[mine], net.core)
+    if fin_oth is not None:
+        y = net.send(fin.at[mine], fin.at[mine], net.ydev)
+        yield
+        y.wait_recv()
+        c1 = net.send(fin_oth.at[mine], fin_oth.at[mine], net.core)
+        yield
+        c1.wait_recv()
+    else:
+        yield
+    c.wait_recv()
+
+
+def reduce_vectors(net, vs, vr, vz):
+    c = net.send(vs.at[0], vr.at[0], net.core)
+    yield
+    c.wait_recv()
+    vs[1] = vs[0] + vr[0]
+    x = net.send(vs.at[1], vr.at[1], net.xdev)
+    yield
+    x.wait_recv()
+    vs[2] = vs[1] + vr[1]
+    vz[net.z] = vs[2]
+    zs = [net.send(vs.at[2], vz.at[net.z], device) for device in net.zdev]
+    yield
+    for z in zs:
+        z.wait_recv()
+    vs[3] = (vz[0] + vz[1]) + (vz[2] + vz[3])
+    k = 3
+    for b, device in enumerate(net.extra):
+        e = net.send(vs.at[k], vr.at[3 + b], device)
+        yield
+        e.wait_recv()
+        vs[k + 1] = vs[k] + vr[3 + b]
+        k += 1
+    y = net.send(vs.at[k], vr.at[2], net.ydev)
+    yield
+    y.wait_recv()
+    vs[k + 1] = vs[k] + vr[2]
+    vs[k + 1, 3:5, :] = vs[k, 3:5, :] + vr[2, 5:7, :]
+
+
 def kernel(
-    tok, seg, pos, cot, whp, wm, wu, wd, vec,
-    out, tg, gd, gu, gm, gh, pg_out, vg,
-    ai, ait, trip, bias, probs, mix, mixt, n1, r1, nb, nbt, hid, gp, gs, bg, bgt, mg, dtrip, acc,
+    dp,
+    tok_h, seg, pos_h, cot_h, hw, mw, uw, dw, vec0,
+    out_h, tg_h, fd_h, fu_h, fm_h, fh_h, fp_h, vg_h,
+    tok, pos, cot, whp, wm, wu, wd, vec,
+    ai, ait, trip, bias, probs, mix, mixt, n1, r1, nbt, hid, gp, gs, bg, bgt, dtrip, acc,
+    gd, gu, gm, gh, gpos, rc, yr, xr, zr, er, rcm, yrm, xrm, zrm, erm, rch, yrh, xrh, zrh, erh,
+    fd, fu, fm, fh, fp, vs, vr, vz,
+    send_sem, recv_sem, local_sem,
 ):
     R, D = tok.shape
     T = pos.shape[0]
@@ -47,25 +226,54 @@
     tiles = R // ROWS
     per = T // ROWS
     lane = lax.broadcasted_iota(jnp.int32, (1, C), 1)
-    t_id = lax.axis_index("tensor")
-
-    def qkv(j):
+    nb, mg = ai, mix
+    net = Net(send_sem, recv_sem, dp)
+    t_id = net.t
+    local = []
+
+    def move(src, dst):
+        copy = pltpu.make_async_copy(src, dst, local_sem.at[len(local)])
+        copy.start()
+        local.append(copy)
+        return copy
+
+    heads_in = [
+        move(hw.at[c, :, p * C : (p + 1) * C], whp.at[0, p, :, c * C : (c + 1) * C]) for p in range(2) for c in range(3)
+    ]
+    tok_in, pos_in = move(tok_h, tok), move(pos_h, pos)
+    merge_in = move(mw, wm.at[0 : D // 2])
+    up_in, down_in = move(uw, wu.at[0]), move(dw, wd.at[0])
+    cot_in = move(cot_h, cot)
+    net.greet()
+    vec[0] = vec0[...]
+    vec_y = net.send(vec0, vec.at[1], net.ydev)
+    for copy in heads_in:
+        copy.wait()
+    get_h = [fetch_direct(net, whp.at[0, p], whp.at[1, p]) for p in range(2)]
+    get_m = fetch_direct(net, wm.at[0 : D // 2], wm.at[D // 2 :])
+    get_u = fetch_shared(net, wu.at[0], wu.at[1])
+    get_d = fetch_shared(net, wd.at[0], wd.at[1])
+    next(get_h[0])
+    next(get_h[1])
+    tok_in.wait()
+    pos_in.wait()
+
+    def enter(j):
         rows = at(j, ROWS)
         x = tok[rows, :].astype(F32) + pos[at(lax.rem(j, per), ROWS), :].astype(F32)
         xb = x.astype(BF16)
         ai[rows, :] = xb
         ait[:, rows] = xb.T
 
-    loop(tiles, qkv)
-
-    def qkv_half(h):
+    loop(tiles, enter)
+
+    def qkv(h, p):
         def body(j):
             rows = at(j, ROWS)
             xb = ai[rows, :]
-            for p in range(2):
-                y = nn(xb, whp[h, p]).astype(BF16)
-                trip[2 * h + p, rows, 0:C] = y[:, 0:C] * 0.125
-                trip[2 * h + p, rows, C:] = y[:, C:]
+            y = nn(xb, whp[h, p]).astype(BF16)
+            trip[2 * h + p, rows, 0:C] = y[:, 0:C] * 0.125
+            trip[2 * h + p, rows, C:] = y[:, C:]
 
         loop(tiles, body)
 
@@ -80,7 +288,7 @@
                 s_id = lax.broadcasted_iota(jnp.int32, (nk, 128), 0)
                 l_id = lax.broadcasted_iota(jnp.int32, (nk, 128), 1) + lo
                 ok = (col[:nk] == row[:, lo : lo + 128]) & (s_id <= l_id)
-                bias[w, :nk, lo : lo + 128] = jnp.where(ok, 0.0, NEG)
+                bias[w, tri(tb), c2 * 128 : c2 * 128 + 128] = jnp.where(ok, 0.0, NEG)
 
     def attend(p, w):
         rows = at(w, T)
@@ -94,22 +302,39 @@
             parts = []
             for a in range(2):
                 qa = jnp.where((lane < HEAD) == (a == 0), q[ts], jnp.zeros((), BF16))
-                s = nt(k[:nk], qa) + bias[w, :nk, ts]
+                s = nt(k[:nk], qa) + bias[w, tri(tb), :]
                 e = jnp.exp(s - jnp.max(s, 0, keepdims=True))
                 pt = (e * (1.0 / jnp.sum(e, 0, keepdims=True))).astype(BF16)
-                probs[w, 2 * p + a, :nk, ts] = pt
+                probs[w, 2 * p + a, tri(tb), :] = pt
                 parts.append(nn(vt[a * HEAD : (a + 1) * HEAD, :nk], pt))
             m = jnp.concatenate(parts, 0).astype(BF16)
             lanes = pl.ds(pl.multiple_of(w * T + tb * ROWS, ROWS), ROWS)
             mixt[cols, lanes] = m
             mix[lanes, cols] = m.T
 
-    def attend_half(h):
-        loop(2 * W, lambda i: attend(2 * h + i // W, lax.rem(i, W)))
-
-    for h in range(2):
-        qkv_half(h)
-        attend_half(h)
+    qkv(0, 0)
+    loop(W, lambda w: attend(0, w))
+    next(get_h[0])
+    merge_in.wait()
+    next(get_m)
+    up_in.wait()
+    next(get_u)
+    qkv(0, 1)
+    loop(W, lambda w: attend(1, w))
+    next(get_h[0])
+    next(get_h[1])
+    down_in.wait()
+    next(get_d)
+    qkv(1, 0)
+    loop(W, lambda w: attend(2, w))
+    next(get_m)
+    next(get_u)
+    next(get_h[1])
+    qkv(1, 1)
+    loop(W, lambda w: attend(3, w))
+    next(get_m)
+    next(get_u)
+    next(get_d)
 
     mb, g1, s1, db, g2, s2 = [vec[0, i : i + 1, :] for i in range(6)]
     acc[...] = jnp.zeros_like(acc)
@@ -149,7 +374,12 @@
         loop(tiles, body)
 
     up(0)
+    next(get_u)
+    next(get_d)
+    vec_y.wait_recv()
     up(1)
+    next(get_d)
+    cot_in.wait()
 
     def down(j):
         rows = at(j, ROWS)
@@ -158,8 +388,8 @@
         z = f - mean(f)
         r = lax.rsqrt(mean(z * z) + 1e-5)
         n2 = z * r
-        out[rows, :] = (n2 * g2 + s2).astype(BF16)
         g = cot[rows, :].astype(F32)
+        cot[rows, :] = (n2 * g2 + s2).astype(BF16)
         e = g * g2
         d = r * (e - mean(e) - n2 * mean(e * n2))
         gs[rows, :] = d
@@ -172,11 +402,30 @@
 
     loop(tiles, down)
 
-    for h in (1, 0):
-        def body(c, h=h):
-            gd[h, :, at(c, D)] = nn(bgt[...], hid[h, :, at(c, D)]).astype(BF16)
-
-        loop(FH // D, body)
+    move(cot, out_h)
+
+    def pieces(g, f, k):
+        return [
+            reduce(net, g.at[c, 0], g.at[c, 1], rc.at[k + c], yr.at[k + c], xr.at[k + c], zr.at[k + c], er.at[k + c], f.at[c])
+            for c in range(FH // D)
+        ]
+
+    red_d, red_u = pieces(gd, fd, 0), pieces(gu, fu, FH // D)
+    red_m = reduce(net, gm.at[0], gm.at[1], rcm.at[0], yrm.at[0], xrm.at[0], zrm.at[0], erm.at[0], fm)
+    red_h = [reduce(net, gh.at[0, i], gh.at[1, i], rch.at[i], yrh.at[i], xrh.at[i], zrh.at[i], erh.at[i], fh.at[i]) for i in range(2)]
+    red_p = reduce(
+        net, gpos.at[t_id], gpos.at[1 - t_id], rcm.at[1], yrm.at[1], xrm.at[1], zrm.at[1], erm.at[1], fp.at[t_id], fp.at[1 - t_id]
+    )
+    red_v = reduce_vectors(net, vs, vr, vz)
+
+    def run(*queue):
+        for g in queue:
+            next(g, None)
+
+    for c in range(FH // D):
+        for h in (1, 0):
+            gd[c, h] = nn(bgt[...], hid[h, :, c * D : (c + 1) * D]).astype(BF16)
+        run(red_d[c])
 
     def hidden_back(j):
         rows = at(j, ROWS)
@@ -189,12 +438,14 @@
                 hid[h, rows, cs] = vb
                 rowsum(3 + 2 * h + c, vb.astype(F32))
 
-    loop(tiles, hidden_back)
-    for h in (1, 0):
-        def body(c, h=h):
-            gu[h, :, at(c, D)] = nn(nbt[...], hid[h, :, at(c, D)]).astype(BF16)
-
-        loop(FH // D, body)
+    run(red_d[0])
+    loop(tiles // 2, hidden_back)
+    run(red_d[1])
+    loop(tiles // 2, lambda j: hidden_back(j + tiles // 2))
+    for c in range(FH // D):
+        for h in (1, 0):
+            gu[c, h] = nn(nbt[...], hid[h, :, c * D : (c + 1) * D]).astype(BF16)
+        run(red_u[c])
 
     def first_back(j):
         rows = at(j, ROWS)
@@ -210,8 +461,17 @@
         rowsum(8, g)
         rowsum(9, d)
 
-    loop(tiles, first_back)
-    gm[...] = nn(mixt[...], bg[...]).astype(BF16)
+    loop(tiles // 2, first_back)
+    run(red_u[0], red_d[0])
+    loop(tiles // 2, lambda j: first_back(j + tiles // 2))
+    run(red_u[1])
+    for h in (1, 0):
+        gm[h] = nn(mixt[h * (D // 2) : (h + 1) * (D // 2), :], bg[...]).astype(BF16)
+    run(red_m, red_d[1], red_d[0])
+    vs[0] = jnp.zeros(vs.shape[1:], F32)
+    for i in range(10):
+        vs[0, i : i + 1, :] = jnp.sum(acc[8 * i : 8 * i + 8, :], 0, keepdims=True)
+    run(red_v)
 
     def attend_back(p, w):
         rows = at(w, T)
@@ -233,7 +493,7 @@
                 doa = jnp.where(mine, do[ts], jnp.zeros((), BF16))
                 qa = jnp.where(mine, q[ts], jnp.zeros((), BF16))
                 inner = jnp.sum(prod[a * HEAD : (a + 1) * HEAD, ts], 0, keepdims=True)
-                pt = probs[w, 2 * p + a, :nk, ts]
+                pt = probs[w, 2 * p + a, tri(tb), :]
                 ds = (pt.astype(F32) * (nt(v[:nk], doa) - inner)).astype(BF16)
                 dqs.append(nn(kt[a * HEAD : (a + 1) * HEAD, :nk], ds))
                 pts.append(pt)
@@ -252,10 +512,18 @@
         dtrip[p, rows, C : 2 * C] = dk.astype(BF16)
         dtrip[p, rows, 2 * C :] = dv.astype(BF16)
 
-    for i in range(2):
-        for h in (1, 0):
-            loop(W, lambda w: attend_back(2 * h + i, w))
-            gh[h, i] = nn(ait[...], dtrip[2 * h + i]).astype(BF16)
+    def back_pair(h, i):
+        loop(W, lambda w: attend_back(2 * h + i, w))
+        gh[h, i] = nn(ait[...], dtrip[2 * h + i]).astype(BF16)
+
+    back_pair(1, 0)
+    run(red_m, red_v, red_u[0], red_d[0], red_d[1])
+    back_pair(0, 0)
+    run(red_h[0], red_v, red_u[1], red_d[0], red_d[1])
+    back_pair(1, 1)
+    run(red_h[0], red_v, red_m, red_u[0], red_d[0], red_d[1])
+    back_pair(0, 1)
+    run(red_h[1], red_v, red_m, red_u[0], red_u[1], red_d[0], red_d[1])
 
     def last(j):
         total = jnp.zeros((ROWS, D), F32)
@@ -264,63 +532,86 @@
             g = gs[rows, :]
             for p in range(4):
                 g += nt(dtrip[p, rows, :], whp[p // 2, p % 2])
-            tg[rows, :] = g
+            gs[rows, :] = g
             total += g
-        pg_out[at(j, ROWS), :] = total.astype(BF16)
+        gpos[j] = total.astype(BF16)
 
     loop(per, last)
-    for i in range(10):
-        vg[i : i + 1, :] = jnp.sum(acc[8 * i : 8 * i + 8, :], 0, keepdims=True)
-
-
-def scratch(R, D, T, FH):
+    move(gs, tg_h)
+    run(red_p)
+    queue = [red_h[0], red_h[1], red_p, red_m, red_v, red_d[0], red_d[1], red_u[0], red_u[1]]
+    done = [(fh.at[0], fh_h.at[0]), (fh.at[1], fh_h.at[1]), (fp, fp_h), (fm, fm_h), (vs.at[vs.shape[0] - 1], vg_h)]
+    done += [(fd.at[c], fd_h.at[c]) for c in range(2)] + [(fu.at[c], fu_h.at[c]) for c in range(2)]
+    while queue:
+        for k in reversed(range(len(queue))):
+            try:
+                next(queue[k])
+            except StopIteration:
+                move(*done[k])
+                del queue[k], done[k]
+    net.finish()
+    for copy in local[len(heads_in) + 6 :]:
+        copy.wait()
+
+
+def scratch(R, D, T, FH, dp):
     W = R // T
     V = pltpu.VMEM
+    area = tri(T // ROWS - 1).stop
+    X = max(1, (dp // 16).bit_length() - 1)
+    NC, DH = FH // D, D // 2
+    sems = 160 + 40 * X
+    assert NC == 2
     return [
-        V((R, D), BF16), V((D, R), BF16), V((4, R, 384), BF16), V((W, T, T), F32), V((W, 8, T, T), BF16),
-        V((R, D), BF16), V((D, R), BF16), V((R, D), F32), V((R, 128), F32), V((R, D), BF16), V((D, R), BF16),
+        V((R, D), BF16), V((T, D), BF16), V((R, D), BF16), V((2, 2, D, 384), BF16), V((D, D), BF16), V((2, D, FH), BF16),
+        V((2, FH, D), BF16), V((2, 8, D), F32),
+        V((R, D), BF16), V((D, R), BF16), V((4, R, 384), BF16), V((W, area, ROWS), F32), V((W, 8, area, ROWS), BF16),
+        V((R, D), BF16), V((D, R), BF16), V((R, D), F32), V((R, 128), F32), V((D, R), BF16),
         V((2, R, FH), BF16), V((2, R, FH), BF16), V((R, D), F32), V((R, D), BF16), V((D, R), BF16),
-        V((R, D), BF16), V((4, R, 384), BF16), V((80, D), F32),
+        V((4, R, 384), BF16), V((80, D), F32),
+        V((NC, 2, D, D), BF16), V((NC, 2, D, D), BF16), V((2, DH, D), BF16), V((2, 2, D, 384), BF16), V((2, T // 2, D), BF16),
+        V((4, 2, DH, D), BF16), V((4, DH, D), BF16), V((4, DH // 2, D), BF16), V((4, 3, D // 16, D), BF16), V((4, X, D // 16, D), BF16),
+        V((2, 2, DH // 2, D), BF16), V((2, DH // 2, D), BF16), V((2, DH // 4, D), BF16), V((2, 3, DH // 16, D), BF16),
+        V((2, X, DH // 16, D), BF16),
+        V((2, 2, DH, 384), BF16), V((2, DH, 384), BF16), V((2, DH // 2, 384), BF16), V((2, 3, D // 16, 384), BF16),
+        V((2, X, D // 16, 384), BF16),
+        V((NC, D, D), BF16), V((NC, D, D), BF16), V((DH, D), BF16), V((2, D, 384), BF16), V((2, T // 2, D), BF16),
+        V((5 + (dp // 16).bit_length() - 1, 16, D), F32), V((3 + X, 16, D), F32), V((4, 16, D), F32),
+        pltpu.SemaphoreType.DMA((sems,)), pltpu.SemaphoreType.DMA((sems,)), pltpu.SemaphoreType.DMA((32,)),
     ]
 
 
-def call(tok, seg, pos, cot, whp, wm, wu, wd, vec):
+def call(dp, tok, seg, pos, cot, hw, mw, uw, dw, vec):
     R, D = tok.shape
     T = pos.shape[0]
-    FH = wu.shape[2]
+    FH = uw.shape[1]
     S = jax.ShapeDtypeStruct
     vm = pl.BlockSpec(memory_space=pltpu.VMEM)
+    hb = pl.BlockSpec(memory_space=pl.ANY)
     outs = [
-        S((R, D), BF16), S((R, D), F32), S((2, D, FH), BF16), S((2, D, FH), BF16), S((D, D), BF16),
-        S((2, 2, D, 384), BF16), S((T, D), BF16), S((16, D), F32),
+        S((R, D), BF16), S((R, D), F32), S((2, D, D), BF16), S((2, D, D), BF16), S((D // 2, D), BF16),
+        S((2, D, 384), BF16), S((2, T // 2, D), BF16), S((16, D), F32),
     ]
     return pl.pallas_call(
-        kernel,
+        functools.partial(kernel, dp),
         out_shape=outs,
-        in_specs=[vm] * 9,
-        out_specs=[vm] * len(outs),
-        scratch_shapes=scratch(R, D, T, FH),
-        compiler_params=pltpu.CompilerParams(vmem_limit_bytes=63 * 2**20),
-    )(tok, seg, pos, cot, whp, wm, wu, wd, vec)
-
-
-def per_device(tok, seg, pos, hw, mw, mb, g1, s1, uw, ub, dw, db, g2, s2, cot):
+        in_specs=[hb, vm, hb, hb, hb, hb, hb, hb, vm],
+        out_specs=[hb] * len(outs),
+        scratch_shapes=scratch(R, D, T, FH, dp),
+        compiler_params=pltpu.CompilerParams(vmem_limit_bytes=VMEM_LIMIT, collective_id=1, has_side_effects=True),
+    )(tok, seg, pos, cot, hw, mw, uw, dw, vec)
+
+
+def per_device(dp, tok, seg, pos, hw, mw, mb, g1, s1, uw, ub, dw, db, g2, s2, cot):
     D = tok.shape[1]
-    half = hw.shape[2]
-    whp = hw.reshape(D, 3, 2, 128).transpose(2, 0, 1, 3).reshape(2, D, 384)
+    T = pos.shape[0]
     vec = jnp.concatenate([v.astype(F32) for v in (mb, g1, s1, db, g2, s2, ub)]).reshape(8, D)
-    swap = lambda v: jnp.stack([v, lax.ppermute(v, "tensor", [(0, 1), (1, 0)])])
-    whp, wm, wu, wd, vec = swap(whp), swap(mw).reshape(2 * half, D), swap(uw), swap(dw), swap(vec)
-    out, tg, gd, gu, gm, gh, pg, vg = call(tok, seg, pos, cot, whp, wm, wu, wd, vec)
-    gm = gm.reshape(2, half, D)
-    pick = lambda v: lax.psum(v[0] + lax.ppermute(v[1], "tensor", [(0, 1), (1, 0)]), "dp").astype(F32)
-    gd, gu, gm, gh = pick(gd), pick(gu), pick(gm), pick(gh)
-    vg_own = lax.psum(vg, "dp")
-    rest = lax.psum(vg, ("dp", "tensor"))
-    ubg = lax.psum(vg[3:5] + lax.ppermute(vg[5:7], "tensor", [(0, 1), (1, 0)]), "dp").reshape(-1)
-    pg = lax.psum(pg.astype(F32), ("dp", "tensor"))
-    hg = gh.reshape(2, D, 3, 128).transpose(1, 2, 0, 3).reshape(D, 3, half)
-    return (out, tg, pg, hg, gm, rest[9], rest[7], rest[8], gu, ubg, gd.T, rest[2], rest[0], rest[1])
+    out, tg, gd, gu, gm, gh, pg, v = call(dp, tok, seg, pos, cot, hw.transpose(1, 0, 2), mw, uw, dw, vec)
+    gd = gd.transpose(0, 2, 1).reshape(-1, D).astype(F32)
+    gu = gu.transpose(1, 0, 2).reshape(D, -1).astype(F32)
+    gh = gh.reshape(2, D, 3, 128).transpose(1, 2, 0, 3).reshape(D, 3, -1).astype(F32)
+    pg = pg.reshape(T, D).astype(F32)
+    return (out, tg, pg, gh, gm.astype(F32), v[9], v[7], v[8], gu, v[3:5].reshape(-1), gd, v[2], v[0], v[1])
 
 
 def solution(mesh):
@@ -329,4 +620,6 @@
            P("tensor", None), P(), P(), P(), rows)
     outs = (rows, rows, P(), P(None, None, "tensor"), P("tensor", None), P(), P(), P(), P(None, "tensor"), P("tensor"),
             P("tensor", None), P(), P(), P())
-    return jax.shard_map(per_device, mesh=mesh, in_specs=ins, out_specs=outs, check_vma=False)
+    return jax.shard_map(
+        functools.partial(per_device, mesh.shape["dp"]), mesh=mesh, in_specs=ins, out_specs=outs, check_vma=False
+    )

time: 359 us -> 151 us (0.42)
  waiting for transfers between devices: 137 us -> 0 us
  blocking collectives: 88.6 us -> 0 us
  Pallas kernels: 71.3 us -> 124 us
  other arithmetic: 19.4 us -> 5.44 us
  between operations: 14.2 us -> 0.71 us
  starting transfers between devices: 12.9 us -> 0 us
  local copies, waits for them, and re-layouts: 15 us -> 19.7 us
    ppermute x10 -> x0, waiting for transfers between devices: 121 us -> none  [the longest x5 60.9 us: per_device(): swap = lambda v: jnp.stack([v, lax.ppermute(v, 'tensor', [(0, 1), (1, 0)])])]
    psum x2 -> x0, blocking collectives: 88.6 us -> none  [the longest x1 56.8 us: per_device(): pg = lax.psum(pg.astype(F32), ('dp', 'tensor'))]
    pallas_call x1, Pallas kernels: 71.3 us -> 124 us  [call(): pl.pallas_call(functools.partial(kernel, dp), out_shape=outs, in_specs=[h...]
    psum x1 -> x0, waiting for transfers between devices: 15.8 us -> none  [per_device(): lax.psum(v[0] + lax.ppermute(v[1], 'tensor', [(0, 1), (1, 0)]), 'dp')]
    ppermute x10 -> x0, starting transfers between devices: 12.8 us -> none  [the longest x5 7.21 us: per_device(): swap = lambda v: jnp.stack([v, lax.ppermute(v, 'tensor', [(0, 1), (1, 0)])])]
    another operation x5 -> x0, other arithmetic: 10.5 us -> none  [per_device(): swap = lambda v: jnp.stack([v, lax.ppermute(v, 'tensor', [(0, 1), (1, 0)])])]
    convert_element_type x0 -> x4, local copies, waits for them, and re-layouts: none -> 5.17 us  [the longest x1 2.88 us: per_device(): gu = gu.transpose(1, 0, 2).reshape(D, -1).astype(F32)]
    unnamed x44 -> x24, local copies, waits for them, and re-layouts: 7.64 us -> 12.6 us
  transfers between devices with their start and end apart: 11 -> 0, of which waited for: 5 -> 0; matrix products, arithmetic and copies ran while one was open for 5% -> 0% of each run, Pallas kernels for 0% -> 0%
where the time goes in v2:
time: 151 us; the launch traced here: 150 us
  Pallas kernels  124 us (82%)
  local copies, waits for them, and re-layouts  19.7 us (13%)
  other arithmetic  5.44 us (4%)
    pallas_call x1, Pallas kernels, call(): pl.pallas_call(functools.partial(kernel, dp), out_shape=outs, in_specs=[h...  124 us
    unnamed x24, local copies, waits for them, and re-layouts  12.6 us
    convert_element_type x1, other arithmetic, per_device(): gd = gd.transpose(0, 2, 1).reshape(-1, D).astype(F32)  3.45 us

profile of v2, /device:TPU:0, one launch (start us, length us, event | category | flops | bytes accessed | tf_op | source)
XLA Modules:
  0.0 150.2 jit_solution(11982821478327955374)
XLA Ops:
  0.7 0.9 dynamic-update-slice
  1.5 0.9 dynamic-update-slice.1
  2.4 0.9 dynamic-update-slice.2
  3.2 0.9 dynamic-update-slice.3
  4.1 0.9 dynamic-update-slice.4
  5.0 0.9 dynamic-update-slice.5
  5.8 0.7 constant_dynamic-update-slice_fusion
  6.5 0.6 reshape.55.vec0
  7.1 124.3 %shard_map.254 = (bf16[1024,512]{1,0:T(8,128)(2,1)}, f32[1024,512]{1,0:T(8,128)}, bf16[2,512,512]{2,1,0:T(8,128)(2,1)}, bf16[2,512,512]{2,1,0:T(8,128)(2,1)}, bf...) custom-call(bf16[1024,512]{1,0:T(8,128)(2,1)} %tok_h.1, ...), custom_call_target="tpu_custom_call" | custom-call | tf_op jit(solution)/shard_map/pallas_call | solution.py:595
  131.5 3.5 %convert_bitcast_fusion = (f32[2,512,512]{1,2,0:T(8,128)S(1)}, f32[512,2,512]{2,0,1:T(8,128)}) fusion(bf16[2,512,512]{2,1,0:T(8,128)(2,1)} %get-tuple-element.29, bf16[2,512,512]{2,1,0:T(8,128)(2,1)} %get-tuple-element.28), kind=kLoop, calls=%fused_computation | loop fusion | flops 1048576 | bytes 6291456 | tf_op jit(solution)/shard_map/convert_element_type | solution.py:610
  134.9 2.9 %copy.36 = f32[512,2,512]{0,2,1:T(8,128)} copy(f32[512,2,512]{2,0,1:T(8,128)} %get-tuple-element.65) | data formatting | bytes 4194304 | tf_op jit(solution)/shard_map/convert_element_type | solution.py:611
  137.8 2.9 %copy.39 = f32[512,1024]{1,0:T(8,128)} copy(f32[512,1024]{0,1:T(8,128)} %bitcast.23) | data formatting | bytes 4194304
  140.7 0.0 copy-start.5
  140.7 0.0 copy-start.2
  140.7 1.8 %copy.37 = f32[2,512,512]{2,1,0:T(8,128)} copy(f32[2,512,512]{1,2,0:T(8,128)S(1)} %get-tuple-element.64) | data formatting | bytes 4194304 | tf_op jit(solution)/shard_map/convert_element_type | solution.py:610
  142.5 0.0 copy-done.5
  142.5 0.6 fusion
  143.1 0.6 copy.40
  143.7 0.0 copy-done.2
  143.7 0.3 copy.34
  144.0 0.2 copy.35
  144.2 0.0 copy-start.3
  144.2 0.0 copy-start.4
  144.2 0.0 copy-start.1
  144.2 1.6 %copy.38 = f32[512,3,256]{2,0,1:T(8,128)} copy(f32[512,3,256]{0,2,1:T(8,128)S(1)} %bitcast.25) | data formatting | bytes 3145728
  145.9 0.0 copy-done.3
  145.9 0.0 copy-start
  145.9 1.1 bitcast_convert_fusion
  147.0 0.0 copy-done.4
  147.0 0.9 convert_element_type.52
  147.9 0.0 copy-done.1
  147.9 1.0 copy.50
  148.8 0.0 copy-done
  148.8 1.3 copy.51
  (2 shorter events, 0.0 us)
Async XLA Ops:
  140.7 1.8 %copy-start.5 = (f32[16,512]{1,0:T(8,128)S(1)}, f32[16,512]{1,0:T(8,128)}, u32[]{:S(2)}) copy-start(f32[16,512]{1,0:T(8,128)} %get-tuple-element.27) | copy-start | bytes 98308
  140.7 3.0 %copy-start.2 = (bf16[2,512,384]{2,1,0:T(8,128)(2,1)S(1)}, bf16[2,512,384]{2,1,0:T(8,128)(2,1)}, u32[]{:S(2)}) copy-start(bf16[2,512,384]{2,1,0:T(8,128)(2,1)} %get-tuple-element.25) | copy-start | bytes 2359300
  144.2 1.6 %copy-start.3 = (bf16[2,256,512]{2,1,0:T(8,128)(2,1)S(1)}, bf16[2,256,512]{2,1,0:T(8,128)(2,1)}, u32[]{:S(2)}) copy-start(bf16[2,256,512]{2,1,0:T(8,128)(2,1)} %get-tuple-element.24) | copy-start | bytes 1572868
  144.2 2.8 %copy-start.4 = (bf16[256,512]{1,0:T(8,128)(2,1)S(1)}, bf16[256,512]{1,0:T(8,128)(2,1)}, u32[]{:S(2)}) copy-start(bf16[256,512]{1,0:T(8,128)(2,1)} %get-tuple-element.26) | copy-start | bytes 786436
  144.2 3.6 %copy-start.1 = (bf16[1024,512]{1,0:T(8,128)(2,1)S(1)}, bf16[1024,512]{1,0:T(8,128)(2,1)}, u32[]{:S(2)}) copy-start(bf16[1024,512]{1,0:T(8,128)(2,1)} %get-tuple-element.80) | copy-start | bytes 3145732
  145.9 3.0 %copy-start = (f32[1024,512]{1,0:T(8,128)S(1)}, f32[1024,512]{1,0:T(8,128)}, u32[]{:S(2)}) copy-start(f32[1024,512]{1,0:T(8,128)} %get-tuple-element.81) | copy-start | bytes 6291460

commit v3 on v2

v3 whole, which is shorter than its diff:
```python
import functools
import jax
import jax.numpy as jnp
from jax import lax
from jax.experimental import pallas as pl
from jax.experimental.pallas import tpu as pltpu
from jax.sharding import PartitionSpec as P

F32, BF16 = jnp.float32, jnp.bfloat16
MESH = pl.DeviceIdType.MESH
FETCH = (("g0", "x"), ("g1", "x"), ("wm", "z"), ("wu0", "z"), ("wu1", "x"), ("wd0", "x"), ("wd1", "y"))
PIECES = (
    ("d0a", "d0", 0, 512, 0, 256, "yxz"),
    ("d0b", "d0", 0, 512, 256, 512, "yxz"),
    ("d1a", "d1", 0, 512, 0, 256, "xzy"),
    ("d1b", "d1", 0, 512, 256, 512, "xzy"),
    ("u0a", "u0", 0, 512, 0, 256, "yxz"),
    ("u0b", "u0", 0, 512, 256, 512, "yxz"),
    ("u1", "u1", 0, 512, 0, 512, "xyz"),
    ("m", "m", 0, 256, 0, 512, "xyz"),
    ("h0a", "h0", 0, 256, 0, 384, "xyz"),
    ("h0b", "h0", 256, 512, 0, 384, "xyz"),
    ("h1a", "h1", 0, 256, 0, 384, "yxz"),
    ("h1b", "h1", 256, 512, 0, 384, "yxz"),
    ("p", "p", 0, 256, 0, 512, "pz"),
)
ORDER = (
    "g0", "wu0", "g1", "wm", "wu1", "enter", "qkv0", "att0", "wd0", "qkv1", "wd1", "g0", "att1", "wu0", "g1", "g0", "wm", "g0",
    "qkv2", "att2", "wu0", "wu1", "g1", "wu0", "wm", "g1", "qkv3", "att3", "wm", "wd0", "merge", "wu1", "up0", "wu1", "wd1",
    "wd0", "up1", "wd1", "wd0", "down", "gd1", "d1a", "d1b", "gd0", "d0a", "d0b", "d1a", "d1b", "hb0", "d0a", "d0b", "hb1", "gu0",
    "u0a", "u0b", "d1a", "gu1", "u1", "d0a", "u0a", "u0b", "fb0", "d1b", "d0b", "u1", "fb1", "d0a", "d1a", "ab0", "u0a", "d0b",
    "ab3", "u0b", "d1b", "d1a", "gm", "m", "gh0", "d0a", "ab2", "d0b", "m", "d1b", "u1", "ab1", "u0a", "d1a", "gh3", "d0a", "u0b",
    "last", "p", "d0b", "m", "u1", "d1b", "gh1", "h1a", "h1b", "d1a", "p", "u0a", "gh2", "h0a", "h0b", "d0a", "u0b", "h1a", "d0b",
    "h1b", "d1a", "m", "h0a", "h0b", "vec", "v", "d0a", "d0b", "d1b", "u1", "v", "d1b", "u0a", "p", "u0b", "h1a", "h0a", "m",
    "h1b", "h0b", "v", "u1", "h0a", "u0a", "p", "h0b", "u0a", "u0b", "m", "h1a", "v", "u0b", "h1b", "h0a", "p", "v", "h0b", "u1",
    "h1a", "m", "u1", "h1b", "m", "h0a", "h0b", "p", "h1a", "h1b", "h0a", "p", "h0b", "h0a", "h1a", "h0b", "h1b", "h1a", "h1b",
)
VMEM_LIMIT = 64 * 2**20 - 2**18
HEAD = 64
ROWS = 256
NEG = -1000000000.0
GELU_A = 0.7978845608028654
GELU_B = GELU_A * 0.044715


def nn(a, b):
    return lax.dot_general(a, b, (((1,), (0,)), ((), ())), preferred_element_type=F32)


def nt(a, b):
    return lax.dot_general(a, b, (((1,), (1,)), ((), ())), preferred_element_type=F32)


def loop(count, body):
    lax.fori_loop(0, count, lambda i, c: (body(i), c)[1], 0)


def at(i, size):
    return pl.ds(pl.multiple_of(i * size, size), size)


def mean(v):
    return jnp.sum(v, -1, keepdims=True) * (1.0 / v.shape[-1])


class Net:
    def __init__(self, send_sem, recv_sem, dp):
        self.send_sem, self.recv_sem, self.sent, self.count = send_sem, recv_sem, [], 0
        i = lax.axis_index("dp")
        self.t = lax.axis_index("tensor")
        self.c = lax.rem(i, 2)
        self.x = lax.rem(i // 2, 2)
        self.z = lax.rem(i // 4, 4)
        self.core = {"dp": i + 1 - 2 * self.c}
        self.xdev = {"dp": i + 2 - 4 * self.x}
        self.ydev = {"tensor": 1 - self.t}
        self.zto = [lax.rem(self.z + s, 4) for s in range(1, 4)]
        self.zdev = [{"dp": i + 4 * (j - self.z)} for j in self.zto]
        self.zpair = {"dp": i + 4 * (1 - 2 * lax.rem(self.z, 2))}
        self.e = lax.rem(i // 2, 8)
        self.eto = [lax.rem(self.e + s, 8) for s in range(1, 8)]
        self.edev = [{"dp": i + 2 * (j - self.e)} for j in self.eto]
        self.xydev = {"dp": i + 2 - 4 * self.x, "tensor": 1 - self.t}
        self.extra = []
        step = 16
        while step < dp:
            bit = lax.rem(i // step, 2)
            self.extra.append({"dp": i + step * (1 - 2 * bit)})
            step *= 2

    def everyone(self):
        more = ([self.xydev] if any("p" in o for *_, o in PIECES) else []) + (self.edev if any("8" in o for *_, o in PIECES) else [self.xdev] + self.zdev)
        return [self.core, self.ydev] + more + self.extra

    def greet(self):
        barrier = pltpu.get_barrier_semaphore()
        for device in self.everyone():
            pl.semaphore_signal(barrier, inc=1, device_id=device, device_id_type=MESH)
        pl.semaphore_wait(barrier, len(self.everyone()))

    def send(self, src, dst, device):
        k = self.count
        self.count += 1
        copy = pltpu.make_async_remote_copy(
            src_ref=src, dst_ref=dst, send_sem=self.send_sem.at[k], recv_sem=self.recv_sem.at[k],
            device_id=device, device_id_type=MESH,
        )
        copy.start()
        self.sent.append(copy)
        return copy

    def finish(self):
        for copy in self.sent:
            copy.wait_send()


def tri(tb):
    return slice(tb * (tb + 1) // 2 * ROWS, (tb + 1) * (tb + 2) // 2 * ROWS)


def part(base, size):
    return pl.ds(pl.multiple_of(base, size), size)


def fetch_direct(net, ready, own, oth):
    half = own.shape[0] // 2
    r = part(net.c * half, half)
    ready.wait()
    y = net.send(own.at[r], oth.at[r], net.ydev)
    yield
    y.wait_recv()
    c = net.send(oth.at[r], oth.at[r], net.core)
    yield
    c.wait_recv()


def fetch_shared(net, ready, own, oth, along):
    q = own.shape[0] // 4
    bit, device = (net.x, net.xdev) if along == "x" else (lax.rem(net.z, 2), net.zpair)
    a = part((2 * net.c + bit) * q, q)
    b = part((2 * net.c + 1 - bit) * q, q)
    ready.wait()
    y = net.send(own.at[a], oth.at[a], net.ydev)
    yield
    y.wait_recv()
    x = net.send(oth.at[a], oth.at[a], device)
    c0 = net.send(oth.at[a], oth.at[a], net.core)
    yield
    x.wait_recv()
    c1 = net.send(oth.at[b], oth.at[b], net.core)
    yield
    c0.wait_recv()
    c1.wait_recv()


class Ready:
    def __init__(self, *copies):
        self.copies = list(copies)

    def wait(self):
        for copy in self.copies:
            copy.wait()
        self.copies = []


def recv_rows(rows, order, extra):
    size, halves, total = rows // 2, 2, rows
    for stage in order:
        if stage == "y":
            total, halves = total + size, 1
        elif stage == "x":
            size //= 2
            total += size * halves
        elif stage == "z":
            size //= 4
            total += 3 * size * halves
        elif stage == "8":
            size //= 8
            total += 7 * size * halves
        elif stage == "p":
            size //= 2
            total, halves = total + 3 * size, 1
    return total + extra * size


def reduce(net, g, own, buf, fin, order):
    rows = g.shape[1]
    oth = 1 - own
    used = [0]
    pending = {0: [], 1: []}

    def take(k):
        used[0] += k
        return buf.at[used[0] - k : used[0]]

    def post(h, base, size, device):
        dst = take(size)
        pending[h is oth].append((net.send(g.at[h, part(base, size)], dst, device), dst))

    def settle(h, base, size, to=None):
        here = part(base, size)
        total = g[h, here, :].astype(F32)
        for copy, dst in pending[h is oth]:
            copy.wait_recv()
            total = total + dst[...].astype(F32)
        pending[h is oth] = []
        if to is None:
            g[h, here, :] = total.astype(BF16)
        else:
            to[here, :] = total.astype(BF16)

    size = rows // 2
    base = net.c * size
    halves = [oth, own]
    for h in halves:
        post(h, (1 - net.c) * size, size, net.core)
    yield
    history = []
    for stage in order:
        history.append((stage, base, size))
        if stage == "y":
            settle(oth, base, size)
            dst = take(size)
            pending[False].append((net.send(g.at[oth, part(base, size)], dst, net.ydev), dst))
            halves = [own]
        elif stage == "p":
            settle(oth, base, size)
            settle(own, base, size)
            size //= 2
            near, far = base + net.x * size, base + (1 - net.x) * size
            for h, start, device in ((oth, far, net.xydev), (oth, near, net.ydev), (own, far, net.xdev)):
                dst = take(size)
                pending[False].append((net.send(g.at[h, part(start, size)], dst, device), dst))
            base, halves = near, [own]
        else:
            for h in halves:
                settle(h, base, size)
            count, to, devices, place = {"x": (2, [1 - net.x], [net.xdev], net.x), "z": (4, net.zto, net.zdev, net.z),
                                         "8": (8, net.eto, net.edev, net.e)}[stage]
            size //= count
            for h in halves:
                for j, device in zip(to, devices):
                    post(h, base + j * size, size, device)
            base = base + place * size
        yield
    last = fin.at[own] if len(fin.shape) == 3 else fin
    settle(own, base, size, last)
    here = part(base, size)
    for device in net.extra:
        dst = take(size)
        copy = net.send(last.at[here], dst, device)
        yield
        copy.wait_recv()
        copy.wait_send()
        net.sent = [o for o in net.sent if o is not copy]
        last[here, :] = (last[here, :].astype(F32) + dst[...].astype(F32)).astype(BF16)
    whole = [last]
    for stage, base, size in reversed(history):
        if stage == "y":
            continue
        devices = {"x": [net.xdev], "z": net.zdev, "8": net.edev, "p": [net.xydev, net.ydev, net.xdev]}[stage]
        copies = [net.send(last.at[here], last.at[here], device) for device in devices]
        yield
        for copy in copies:
            copy.wait_recv()
        here = part(base, size)
        if stage == "p":
            whole = [fin.at[own], fin.at[oth]]
    copies = [net.send(f.at[here], f.at[here], net.core) for f in whole]
    yield
    for copy in copies:
        copy.wait_recv()


def reduce_vectors(net, vs, vr, vz):
    c = net.send(vs.at[0], vr.at[0], net.core)
    yield
    c.wait_recv()
    vs[1] = vs[0] + vr[0]
    x = net.send(vs.at[1], vr.at[1], net.xdev)
    yield
    x.wait_recv()
    vs[2] = vs[1] + vr[1]
    vz[net.z] = vs[2]
    zs = [net.send(vs.at[2], vz.at[net.z], device) for device in net.zdev]
    yield
    for z in zs:
        z.wait_recv()
    vs[3] = (vz[0] + vz[1]) + (vz[2] + vz[3])
    k = 3
    for b, device in enumerate(net.extra):
        e = net.send(vs.at[k], vr.at[3 + b], device)
        yield
        e.wait_recv()
        vs[k + 1] = vs[k] + vr[3 + b]
        k += 1
    y = net.send(vs.at[k], vr.at[2], net.ydev)
    yield
    y.wait_recv()
    vs[k + 1] = vs[k] + vr[2]
    vs[k + 1, 3:5, :] = vs[k, 3:5, :] + vr[2, 5:7, :]


REACH = 256


def span(j):
    return max(0, (j + 1) * 128 - REACH - 128), (j + 1) * 128


def strip(j):
    start = sum(span(i)[1] - span(i)[0] for i in range(j))
    return slice(start, start + span(j)[1] - span(j)[0])


def kernel(
    dp,
    tok_h, seg, pos_h, cot_h, hw, mw, uw, dw, v0, v1, v2, v3, v4, v5, v6,
    out_h, tg_h, fd_h, fu_h, fm_h, fh_h, fp_h, vg_h,
    tok, pos, cot, whp, wm, wu, wd, vec,
    ai, ait, trip, bias, probs, mix, mixt, n1, r1, nbt, hid, gp, gs, bg, bgt, dtrip, acc,
    gd, gu, gm, gh, gpos, fd, fu, fm, fh, fp, vs, vr, vz,
    send_sem, recv_sem, local_sem, *bufs,
):
    R, D = tok.shape
    T = pos.shape[0]
    W = R // T
    FH = wu.shape[2]
    C = 128
    tiles = R // ROWS
    per = T // ROWS
    lane = lax.broadcasted_iota(jnp.int32, (1, C), 1)
    nb, mg = ai, mix
    net = Net(send_sem, recv_sem, dp)
    t_id = net.t
    local = []

    def move(src, dst):
        copy = pltpu.make_async_copy(src, dst, local_sem.at[len(local)])
        copy.start()
        local.append(copy)
        return copy

    heads_in = [
        Ready(*[move(hw.at[c, :, p * C : (p + 1) * C], whp.at[0, p, :, c * C : (c + 1) * C]) for c in range(3)])
        for p in range(2)
    ]
    rows_in = Ready(move(tok_h, tok), move(pos_h, pos))
    merge_in, up_in, down_in = Ready(move(mw, wm.at[0 : D // 2])), Ready(move(uw, wu.at[0])), Ready(move(dw, wd.at[0]))
    cot_in = Ready(move(cot_h, cot))
    inward = len(local)
    net.greet()
    for k, v in enumerate((v0, v1, v2, v3, v4, v5)):
        vec[0, k : k + 1, :] = v[...].astype(F32).reshape(1, D)
    for k in range(FH // D):
        vec[0, 6 + k : 7 + k, :] = v6[k * D : (k + 1) * D].astype(F32).reshape(1, D)
    mb, g1, s1, db, g2, s2 = [vec[0, i : i + 1, :] for i in range(6)]
    vec_y = net.send(vec.at[0], vec.at[1], net.ydev)

    steps = {}
    halves = {"g0": (heads_in[0], whp.at[0, 0], whp.at[1, 0]), "g1": (heads_in[1], whp.at[0, 1], whp.at[1, 1])}
    halves["wm"] = (merge_in, wm.at[0 : D // 2], wm.at[D // 2 :])
    for k in range(2):
        r = slice(k * D // 2, (k + 1) * D // 2)
        halves[f"wu{k}"] = (up_in, wu.at[0, r], wu.at[1, r])
        r = slice(k * FH // 2, (k + 1) * FH // 2)
        halves[f"wd{k}"] = (down_in, wd.at[0, r], wd.at[1, r])
    for name, way in FETCH:
        steps[name] = fetch_direct(net, *halves[name]) if way == "y" else fetch_shared(net, *halves[name], way)
    whole = {"m": (gm, fm, fm_h), "p": (gpos, fp, fp_h)}
    for k in range(2):
        whole[f"d{k}"] = (gd.at[k], fd.at[k], fd_h.at[k])
        whole[f"u{k}"] = (gu.at[k], fu.at[k], fu_h.at[k])
        whole[f"h{k}"] = (gh.at[k], fh.at[k], fh_h.at[k])
    ends = {"v": (vs.at[vs.shape[0] - 1], vg_h)}
    for (name, key, r0, r1_, c0, c1, order), buf in zip(PIECES, bufs):
        g, f, f_h = whole[key]
        if key != "p":
            g, f, f_h = g.at[:, r0:r1_, c0:c1], f.at[r0:r1_, c0:c1], f_h.at[r0:r1_, c0:c1]
        steps[name] = reduce(net, g, t_id if key == "p" else 0, buf, f, order)
        ends[name] = (f, f_h)
    steps["v"] = reduce_vectors(net, vs, vr, vz)
    def enter(j):
        rows = at(j, ROWS)
        x = tok[rows, :].astype(F32) + pos[at(lax.rem(j, per), ROWS), :].astype(F32)
        xb = x.astype(BF16)
        ai[rows, :] = xb
        ait[:, rows] = xb.T

    def seg_enter():
        rows_in.wait()
        loop(tiles, enter)
        masks()

    def qkv(h, p):
        every = [slice(j * ROWS, (j + 1) * ROWS) for j in range(tiles)]
        ys = [nn(ai[rows, :], whp[h, p]).astype(BF16) for rows in every]
        for rows, y in zip(every, ys):
            trip[2 * h + p, rows, 0:C] = y[:, 0:C] * 0.125
            trip[2 * h + p, rows, C:] = y[:, C:]

    def masks():
        for w in range(W):
            row = seg[pl.ds(t_id * W + w, 1), :].astype(F32)
            col = jnp.broadcast_to(row, (C, T)).T
            for j in range(T // C):
                lo, hi = span(j)
                s_id = lax.broadcasted_iota(jnp.int32, (hi - lo, C), 0) + lo
                l_id = lax.broadcasted_iota(jnp.int32, (hi - lo, C), 1) + j * C
                ok = (col[lo:hi] == row[:, j * C : (j + 1) * C]) & (s_id <= l_id)
                bias[w, strip(j), :] = jnp.where(ok, 0.0, NEG)

    def attend(p, ws):
        zero = jnp.zeros((), BF16)
        first = lane < HEAD
        strips = range(T // C)
        cols = at(p, C)
        ss, bs, vts, ms, pts = {}, {}, {}, {}, {}
        for w in ws:
            rows = at(w, T)
            q = trip[p, rows, 0:C]
            k = trip[p, rows, C : 2 * C]
            for j in strips:
                lo, hi = span(j)
                qj = q[j * C : (j + 1) * C]
                ss[w, j] = nt(k[lo:hi], jnp.concatenate([jnp.where(first, qj, zero), jnp.where(first, zero, qj)], 0))
                bs[w, j] = bias[w, strip(j), :]
            vts[w] = trip[p, rows, 2 * C :].T
        for w in ws:
            for j in strips:
                halves = []
                for a in range(2):
                    v = ss[w, j][:, a * C : (a + 1) * C] + bs[w, j]
                    e = jnp.exp(v - jnp.max(v, 0, keepdims=True))
                    halves.append((e * (1.0 / jnp.sum(e, 0, keepdims=True))).astype(BF16))
                pts[w, j] = jnp.concatenate(halves, 1)
            for j in strips:
                lo, hi = span(j)
                m = nn(vts[w][:, lo:hi], pts[w, j])
                ms[w, j] = jnp.concatenate([m[:HEAD, :C], m[HEAD:, C:]], 0).astype(BF16)
        for w in ws:
            rows = at(w, T)
            for j in strips:
                probs[w, p, strip(j), :] = pts[w, j]
            m = jnp.concatenate([ms[w, j] for j in strips], 1)
            mixt[cols, rows] = m
            mix[rows, cols] = m.T

    def rowsum(i, v):
        acc[pl.ds(8 * i, 8), :] += jnp.sum(v.reshape(-1, 8, v.shape[-1]), 0)

    def merge(jj):
        both = [at(2 * jj + i, ROWS) for i in range(2)]
        xs = [
            tok[rows, :].astype(F32) + pos[at(lax.rem(2 * jj + i, per), ROWS), :].astype(F32) + mb for i, rows in enumerate(both)
        ]
        fs = [x + nn(mix[rows, :], wm[...]) for x, rows in zip(xs, both)]
        zs = [f - mean(f) for f in fs]
        rs = [lax.rsqrt(mean(z * z) + 1e-5) for z in zs]
        ns = [z * r for z, r in zip(zs, rs)]
        ys = [(n * g1 + s1).astype(BF16) for n in ns]
        for rows, n, r, y in zip(both, ns, rs, ys):
            n1[rows, :] = n
            r1[rows, :] = jnp.broadcast_to(r, (ROWS, 128))
            nb[rows, :] = y
            nbt[:, rows] = y.T

    def up(h):
        def body(j):
            rows = at(j, ROWS)
            x = nb[rows, :]
            chunks = [slice(c * D // 2, (c + 1) * D // 2) for c in range(2 * FH // D)]
            vs = [nn(x, wu[h, :, cs]) + vec[h, 6 + cs.start // D : 7 + cs.start // D, cs.start % D : cs.start % D + D // 2] for cs in chunks]
            hs, ps = [], []
            for v in vs:
                v2 = v * v
                th = jnp.tanh(v * (GELU_A + GELU_B * v2))
                half = 0.5 + 0.5 * th
                hv = v * half
                hs.append(hv.astype(BF16))
                ps.append((half + hv * (1.0 - th) * (GELU_A + 3.0 * GELU_B * v2)).astype(BF16))
            for cs, hv, pv in zip(chunks, hs, ps):
                hid[h, rows, cs] = hv
                gp[h, rows, cs] = pv

        loop(tiles, body)

    def down(jj):
        both = [at(2 * jj + i, ROWS) for i in range(2)]
        gvs = [cot[rows, :] for rows in both]
        fs = [n1[rows, :] * g1 + (s1 + db) + (nn(hid[0, rows, :], wd[0]) + nn(hid[1, rows, :], wd[1])) for rows in both]
        todo = []
        for rows, f, g in zip(both, fs, gvs):
            z = f - mean(f)
            r = lax.rsqrt(mean(z * z) + 1e-5)
            n2 = z * r
            g = g.astype(F32)
            e = g * g2
            d = r * (e - mean(e) - n2 * mean(e * n2))
            todo.append((rows, (n2 * g2 + s2).astype(BF16), d, d.astype(BF16), g * n2, g))
        for rows, o, d, b, _, _ in todo:
            cot[rows, :] = o
            gs[rows, :] = d
            bg[rows, :] = b
            bgt[:, rows] = b.T
        for _, _, d, _, gn, g in todo:
            rowsum(0, gn)
            rowsum(1, g)
            rowsum(2, d)

    def seg_down():
        cot_in.wait()
        loop(tiles // 2, down)
        move(cot, out_h)

    def grad_down(c):
        for h in (1, 0):
            gd[c, h] = nn(bgt[...], hid[h, :, c * D : (c + 1) * D]).astype(BF16)

    def hidden_back(j):
        rows = at(j, ROWS)
        b = bg[rows, :]
        todo = [(h, c) for h in range(2) for c in range(FH // D)]
        dh = {k: nt(b, wd[k[0], k[1] * D : (k[1] + 1) * D, :]) for k in todo}
        vb = {(h, c): (dh[h, c] * gp[h, rows, c * D : (c + 1) * D].astype(F32)).astype(BF16) for h, c in todo}
        for h, c in todo:
            hid[h, rows, c * D : (c + 1) * D] = vb[h, c]
        for h, c in todo:
            rowsum(3 + 2 * h + c, vb[h, c].astype(F32))

    def grad_up(c):
        for h in (1, 0):
            gu[c, h] = nn(nbt[...], hid[h, :, c * D : (c + 1) * D]).astype(BF16)

    def first_back(jj):
        both = [at(2 * jj + i, ROWS) for i in range(2)]
        gg = [gs[rows, :] + (nt(hid[0, rows, :], wu[0]) + nt(hid[1, rows, :], wu[1])) for rows in both]
        nns = [n1[rows, :] for rows in both]
        rr = [r1[rows, 0:1] for rows in both]
        ds = []
        for g, n, r in zip(gg, nns, rr):
            e = g * g1
            ds.append(r * (e - mean(e) - n * mean(e * n)))
        bs = [d.astype(BF16) for d in ds]
        ms = [nt(b, wm[...]).astype(BF16) for b in bs]
        for rows, d, b, m in zip(both, ds, bs, ms):
            gs[rows, :] = d
            bg[rows, :] = b
            mg[rows, :] = m
        for g, n, d in zip(gg, nns, ds):
            rowsum(7, g * n)
            rowsum(8, g)
            rowsum(9, d)

    def grad_merge():
        for h in (1, 0):
            gm[h] = nn(mixt[h * (D // 2) : (h + 1) * (D // 2), :], bg[...]).astype(BF16)

    def vectors():
        vs[0] = jnp.zeros(vs.shape[1:], F32)
        for i in range(10):
            vs[0, i : i + 1, :] = jnp.sum(acc[8 * i : 8 * i + 8, :], 0, keepdims=True)

    def attend_back(p, ws):
        zero = jnp.zeros((), BF16)
        first = lane < HEAD
        strips = range(T // C)
        cols = at(p, C)
        both = lambda x: jnp.concatenate([jnp.where(first, x, zero), jnp.where(first, zero, x)], 0)
        cut = lambda x, j, s: x[s * C - span(j)[0] : (s + 1) * C - span(j)[0], :]
        users = [[j for j in strips if span(j)[0] <= s * C < span(j)[1]] for s in strips]
        dps, pts, dds, dvs, kts, qqs, prods, dss, dks, ms = [{} for _ in range(10)]
        for w in ws:
            rows = at(w, T)
            v = trip[p, rows, 2 * C :]
            do = mg[rows, cols]
            q = trip[p, rows, 0:C]
            for j in strips:
                dds[w, j] = both(do[j * C : (j + 1) * C])
                dps[w, j] = nt(v[span(j)[0] : span(j)[1]], dds[w, j])
                pts[w, j] = probs[w, p, strip(j), :]
                qqs[w, j] = both(q[j * C : (j + 1) * C])
            prods[w] = do.T.astype(F32) * mixt[cols, rows].astype(F32)
            kts[w] = trip[p, rows, C : 2 * C].T
        for w in ws:
            for s in strips:
                js = users[s]
                dvs[w, s] = nn(jnp.concatenate([cut(pts[w, j], j, s) for j in js], 1), jnp.concatenate([dds[w, j] for j in js], 0))
            for j in strips:
                ts = slice(j * C, (j + 1) * C)
                ds = []
                for a in range(2):
                    cs = slice(a * C, (a + 1) * C)
                    inner = jnp.sum(prods[w][a * HEAD : (a + 1) * HEAD, ts], 0, keepdims=True)
                    ds.append((pts[w, j][:, cs].astype(F32) * (dps[w, j][:, cs] - inner)).astype(BF16))
                dss[w, j] = jnp.concatenate(ds, 1)
            for j in strips:
                m = nn(kts[w][:, span(j)[0] : span(j)[1]], dss[w, j])
                ms[w, j] = (jnp.concatenate([m[:HEAD, :C], m[HEAD:, C:]], 0) * 0.125).astype(BF16)
            for s in strips:
                js = users[s]
                dks[w, s] = nn(jnp.concatenate([cut(dss[w, j], j, s) for j in js], 1), jnp.concatenate([qqs[w, j] for j in js], 0))
        for w in ws:
            rows = at(w, T)
            dtrip[p, rows, 0:C] = jnp.concatenate([ms[w, j] for j in strips], 1).T
            for s in strips:
                lanes = pl.ds(pl.multiple_of(w * T + s * C, C), C)
                dtrip[p, lanes, C : 2 * C] = dks[w, s].astype(BF16)
                dtrip[p, lanes, 2 * C :] = dvs[w, s].astype(BF16)

    def last(j):
        total = jnp.zeros((ROWS, D), F32)
        for w in range(W):
            rows = pl.ds(pl.multiple_of(w * T + j * ROWS, ROWS), ROWS)
            g = gs[rows, :]
            for p in range(4):
                g += nt(dtrip[p, rows, :], whp[p // 2, p % 2])
            gs[rows, :] = g
            total += g
        gpos[j] = total.astype(BF16)

    def seg_last():
        loop(per, last)
        move(gs, tg_h)

    assert tiles == 4

    def half(body, k):
        loop(tiles // 2, lambda j: body(j + k * (tiles // 2)))

    def seg_up1():
        vec_y.wait_recv()
        up(1)

    acc[...] = jnp.zeros_like(acc)
    work = {"enter": seg_enter, "merge": lambda: loop(tiles // 2, merge), "up0": lambda: up(0), "up1": seg_up1, "down": seg_down}
    work.update({"gm": grad_merge, "vec": vectors, "last": seg_last})
    for p in range(4):
        work[f"qkv{p}"] = lambda p=p: qkv(p // 2, p % 2)
        work[f"att{p}"] = lambda p=p: attend(p, range(W))
        work[f"ab{p}"] = lambda p=p: attend_back(p, range(W))
        work[f"gh{p}"] = lambda p=p: gh.__setitem__((p % 2, p // 2), nn(ait[...], dtrip[p]).astype(BF16))
    for k in range(2):
        work[f"gd{k}"] = lambda k=k: grad_down(k)
        work[f"gu{k}"] = lambda k=k: grad_up(k)
        work[f"hb{k}"] = lambda k=k: half(hidden_back, k)
        work[f"fb{k}"] = lambda k=k: first_back(k)
    for name in ORDER:
        if name in work:
            work[name]()
            continue
        try:
            next(steps[name])
        except StopIteration:
            del steps[name]
            if name in ends:
                move(*ends[name])
    for name in list(steps):
        for _ in steps[name]:
            pass
        if name in ends:
            move(*ends[name])
    net.finish()
    for copy in local[inward:]:
        copy.wait()


def scratch(R, D, T, FH, dp):
    W = R // T
    V = pltpu.VMEM
    area = strip(T // 128 - 1).stop
    X = max(1, (dp // 16).bit_length() - 1)
    NC, DH = FH // D, D // 2
    sems = 240 + 40 * X
    assert NC == 2
    return [
        V((R, D), BF16), V((T, D), BF16), V((R, D), BF16), V((2, 2, D, 384), BF16), V((D, D), BF16), V((2, D, FH), BF16),
        V((2, FH, D), BF16), V((2, 8, D), F32),
        V((R, D), BF16), V((D, R), BF16), V((4, R, 384), BF16), V((W, area, 128), F32), V((W, 4, area, 256), BF16),
        V((R, D), BF16), V((D, R), BF16), V((R, D), F32), V((R, 128), F32), V((D, R), BF16),
        V((2, R, FH), BF16), V((2, R, FH), BF16), V((R, D), F32), V((R, D), BF16), V((D, R), BF16),
        V((4, R, 384), BF16), V((80, D), F32),
        V((NC, 2, D, D), BF16), V((NC, 2, D, D), BF16), V((2, DH, D), BF16), V((2, 2, D, 384), BF16), V((2, T // 2, D), BF16),
        V((NC, D, D), BF16), V((NC, D, D), BF16), V((DH, D), BF16), V((2, D, 384), BF16), V((2, T // 2, D), BF16),
        V((5 + (dp // 16).bit_length() - 1, 16, D), F32), V((3 + X, 16, D), F32), V((4, 16, D), F32),
        pltpu.SemaphoreType.DMA((sems,)), pltpu.SemaphoreType.DMA((sems,)), pltpu.SemaphoreType.DMA((40,)),
    ] + [V((recv_rows(b - a, order, (dp // 16).bit_length() - 1), d - c), BF16) for _, _, a, b, c, d, order in PIECES]


def call(dp, tok, seg, pos, cot, hw, mw, uw, dw, *vecs):
    R, D = tok.shape
    T = pos.shape[0]
    FH = uw.shape[1]
    S = jax.ShapeDtypeStruct
    vm = pl.BlockSpec(memory_space=pltpu.VMEM)
    hb = pl.BlockSpec(memory_space=pl.ANY)
    outs = [
        S((R, D), BF16), S((R, D), F32), S((2, D, D), BF16), S((2, D, D), BF16), S((D // 2, D), BF16),
        S((2, D, 384), BF16), S((2, T // 2, D), BF16), S((16, D), F32),
    ]
    return pl.pallas_call(
        functools.partial(kernel, dp),
        out_shape=outs,
        in_specs=[hb, vm, hb, hb, hb, hb, hb, hb] + [vm] * 7,
        out_specs=[hb] * len(outs),
        scratch_shapes=scratch(R, D, T, FH, dp),
        compiler_params=pltpu.CompilerParams(vmem_limit_bytes=VMEM_LIMIT, collective_id=1, has_side_effects=True),
    )(tok, seg, pos, cot, hw, mw, uw, dw, *vecs)


def widen(out_h, tg_h, fd_h, fu_h, fm_h, fh_h, fp_h, v, out, tg, pg_o, hg_o, gm_o, gu_o, gd_o, mb, g1, s1, ub, db, g2, s2,
          fd, fu, fm, fh, fp, tgv, outv, pg, hg, gm, gu, gd, sem, osem):
    D = fm.shape[1]
    pairs = [(fd_h, fd), (fu_h, fu), (fh_h, fh), (fm_h, fm), (fp_h, fp), (tg_h, tgv), (out_h, outv)]
    ins = [pltpu.make_async_copy(a, b, sem.at[k]) for k, (a, b) in enumerate(pairs)]
    for copy in ins:
        copy.start()
    outs = []

    def leave(src, dst):
        copy = pltpu.make_async_copy(src, dst, osem.at[len(outs)])
        copy.start()
        outs.append(copy)

    for row, o in ((9, mb), (7, g1), (8, s1), (2, db), (0, g2), (1, s2)):
        o[...] = v[row, :]
    for k in range(2):
        ub[k * D : (k + 1) * D] = v[3 + k, :]
    ins[0].wait()
    for c in range(2):
        for r in range(2):
            rows = slice(c * D + r * (D // 2), c * D + (r + 1) * (D // 2))
            gd[rows, :] = fd[c, :, r * (D // 2) : (r + 1) * (D // 2)].T.astype(F32)
        leave(gd.at[c * D : (c + 1) * D], gd_o.at[c * D : (c + 1) * D])
    ins[1].wait()
    for r in range(2):
        rows = slice(r * (D // 2), (r + 1) * (D // 2))
        for c in range(2):
            gu[rows, c * D : (c + 1) * D] = fu[c, rows, :].astype(F32)
        leave(gu.at[rows], gu_o.at[rows])
    ins[2].wait()
    for k in range(3):
        for p in range(2):
            hg[k, :, p * 128 : (p + 1) * 128] = fh[p, :, k * 128 : (k + 1) * 128].astype(F32)
        leave(hg.at[k], hg_o.at[k])
    ins[3].wait()
    gm[...] = fm[...].astype(F32)
    leave(gm, gm_o)
    ins[4].wait()
    for k in range(2):
        rows = slice(k * (D // 2), (k + 1) * (D // 2))
        pg[rows, :] = fp[k].astype(F32)
    leave(pg, pg_o)
    ins[5].wait()
    leave(tgv, tg)
    ins[6].wait()
    leave(outv, out)
    for copy in outs:
        copy.wait()


def finish(out, tg, fd, fu, fm, fh, fp, v):
    D = fm.shape[1]
    half = fm.shape[0]
    S, V = jax.ShapeDtypeStruct, pltpu.VMEM
    shapes = [(2 * half, D), (3, D, half), (half, D), (D, 2 * D), (2 * D, D)]
    hb = pl.BlockSpec(memory_space=pl.ANY)
    vm = pl.BlockSpec(memory_space=pltpu.VMEM)
    return pl.pallas_call(
        widen,
        out_shape=[S(out.shape, BF16), S(tg.shape, F32)] + [S(v, F32) for v in shapes]
        + [S((n,), F32) for n in (D, D, D, 2 * D, D, D, D)],
        in_specs=[hb] * 7 + [vm],
        out_specs=[hb] * 7 + [vm] * 7,
        scratch_shapes=[V(v.shape, BF16) for v in (fd, fu, fm, fh, fp)] + [V(tg.shape, F32), V(out.shape, BF16)] + [V(v, F32) for v in shapes]
        + [pltpu.SemaphoreType.DMA((7,)), pltpu.SemaphoreType.DMA((16,))],
        compiler_params=pltpu.CompilerParams(vmem_limit_bytes=VMEM_LIMIT),
    )(out, tg, fd, fu, fm, fh, fp, v)


def per_device(dp, tok, seg, pos, hw, mw, mb, g1, s1, uw, ub, dw, db, g2, s2, cot):
    out, tg, fd, fu, fm, fh, fp, v = call(dp, tok, seg, pos, cot, hw.transpose(1, 0, 2), mw, uw, dw, mb, g1, s1, db, g2, s2, ub)
    out, tg, pg, gh, gm, gu, gd, *vs = finish(out, tg, fd, fu, fm, fh, fp, v)
    mb, g1, s1, ub, db, g2, s2 = vs
    return (out, tg, pg, gh.transpose(1, 0, 2), gm, mb, g1, s1, gu, ub, gd, db, g2, s2)


def solution(mesh):
    rows = P(("dp", "tensor"), None)
    ins = (rows, P("dp", None), P(), P(None, None, "tensor"), P("tensor", None), P(), P(), P(), P(None, "tensor"), P("tensor"),
           P("tensor", None), P(), P(), P(), rows)
    outs = (rows, rows, P(), P(None, None, "tensor"), P("tensor", None), P(), P(), P(), P(None, "tensor"), P("tensor"),
            P("tensor", None), P(), P(), P())
    return jax.shard_map(
        functools.partial(per_device, mesh.shape["dp"]), mesh=mesh, in_specs=ins, out_specs=outs, check_vma=False
    )
```

time: 151 us -> 110 us (0.73)
  local copies, waits for them, and re-layouts: 19.7 us -> 0 us
  Pallas kernels: 124 us -> 109 us
  other arithmetic: 5.44 us -> 0 us
    pallas_call x1, Pallas kernels: 124 us -> 102 us  [call(): pl.pallas_call(functools.partial(kernel, dp), out_shape=outs, in_specs=[h...]
    unnamed x24 -> x0, local copies, waits for them, and re-layouts: 12.6 us -> none
    pallas_call x0 -> x1, Pallas kernels: none -> 6.99 us  [finish(): pl.pallas_call(widen, out_shape=[S(out.shape, BF16), S(tg.shape, F32)] +...]
    convert_element_type x3 -> x0, other arithmetic: 5.44 us -> none  [the longest x1 3.45 us: per_device(): gd = gd.transpose(0, 2, 1).reshape(-1, D).astype(F32)]
    convert_element_type x4 -> x0, local copies, waits for them, and re-layouts: 5.17 us -> none  [the longest x1 2.88 us: per_device(): gu = gu.transpose(1, 0, 2).reshape(D, -1).astype(F32)]
where the time goes in v3:
time: 110 us
  Pallas kernels  109 us (99%)
    pallas_call x1, Pallas kernels, call(): pl.pallas_call(functools.partial(kernel, dp), out_shape=outs, in_specs=[h...  102 us
    pallas_call x1, Pallas kernels, finish(): pl.pallas_call(widen, out_shape=[S(out.shape, BF16), S(tg.shape, F32)] +...  6.99 us

profile of v3, /device:TPU:0, one launch (start us, length us, event | category | flops | bytes accessed | tf_op | source)
XLA Modules:
  0.0 109.8 jit_solution(15376904304387903615)
XLA Ops:
  0.7 102.0 %shard_map.254 = (bf16[1024,512]{1,0:T(8,128)(2,1)}, f32[1024,512]{1,0:T(8,128)}, bf16[2,512,512]{2,1,0:T(8,128)(2,1)}, bf16[2,512,512]{2,1,0:T(8,128)(2,1)}, bf...) custom-call(bf16[1024,512]{1,0:T(8,128)(2,1)} %tok_h.1, ...), custom_call_target="tpu_custom_call" | custom-call | tf_op jit(solution)/shard_map/pallas_call | solution.py:701
  102.7 7.0 %shard_map.255 = (bf16[1024,512]{1,0:T(8,128)(2,1)}, f32[1024,512]{1,0:T(8,128)}, f32[512,512]{1,0:T(8,128)}, f32[3,512,256]{2,1,0:T(8,128)}, f32[256,512]{1,0:T...) custom-call(bf16[1024,512]{1,0:T(8,128)(2,1)} %get-tuple-element.36., ...), custom_call_target="tpu_custom_call" | custom-call | tf_op jit(solution)/shard_map/pallas_call | solution.py:769

commit v4 on v3

--- a/solution.py
+++ b/solution.py
@@ -8,34 +8,44 @@
 
 F32, BF16 = jnp.float32, jnp.bfloat16
 MESH = pl.DeviceIdType.MESH
-FETCH = (("g0", "x"), ("g1", "x"), ("wm", "z"), ("wu0", "z"), ("wu1", "x"), ("wd0", "x"), ("wd1", "y"))
+FETCH = (
+    ("wm", "wm", 0, 256, "x"),
+    ("g0", "g0", 0, 512, "e"),
+    ("wd", "wd", 0, 1024, "e"),
+    ("g1", "g1", 0, 512, "e"),
+    ("wu0", "wu", 0, 256, "x"),
+    ("wu1", "wu", 256, 512, "y"),
+)
 PIECES = (
-    ("d0a", "d0", 0, 512, 0, 256, "yxz"),
-    ("d0b", "d0", 0, 512, 256, 512, "yxz"),
-    ("d1a", "d1", 0, 512, 0, 256, "xzy"),
-    ("d1b", "d1", 0, 512, 256, 512, "xzy"),
-    ("u0a", "u0", 0, 512, 0, 256, "yxz"),
-    ("u0b", "u0", 0, 512, 256, 512, "yxz"),
-    ("u1", "u1", 0, 512, 0, 512, "xyz"),
-    ("m", "m", 0, 256, 0, 512, "xyz"),
-    ("h0a", "h0", 0, 256, 0, 384, "xyz"),
-    ("h0b", "h0", 256, 512, 0, 384, "xyz"),
-    ("h1a", "h1", 0, 256, 0, 384, "yxz"),
-    ("h1b", "h1", 256, 512, 0, 384, "yxz"),
+    ("d0", "d0", 0, 512, 0, 256, "xaby"),
+    ("u0", "u0", 0, 512, 0, 256, "yxz"),
+    ("d1", "d0", 0, 512, 256, 512, "xaby"),
+    ("u1", "u0", 0, 512, 256, 512, "xyab"),
+    ("d2", "d1", 0, 512, 0, 256, "xyz"),
+    ("u2", "u1", 0, 512, 0, 256, "xyab"),
+    ("d3", "d1", 0, 512, 256, 512, "yxz"),
+    ("u3", "u1", 0, 512, 256, 512, "ayxb"),
+    ("m", "m", 0, 256, 0, 512, "ayxb"),
     ("p", "p", 0, 256, 0, 512, "pz"),
+    ("h0a", "h0", 0, 256, 0, 384, "xyab"),
+    ("h0b", "h0", 256, 512, 0, 384, "yabx"),
+    ("h1a", "h1", 0, 256, 0, 384, "yzx"),
+    ("h1b", "h1", 256, 512, 0, 384, "xyz"),
 )
 ORDER = (
-    "g0", "wu0", "g1", "wm", "wu1", "enter", "qkv0", "att0", "wd0", "qkv1", "wd1", "g0", "att1", "wu0", "g1", "g0", "wm", "g0",
-    "qkv2", "att2", "wu0", "wu1", "g1", "wu0", "wm", "g1", "qkv3", "att3", "wm", "wd0", "merge", "wu1", "up0", "wu1", "wd1",
-    "wd0", "up1", "wd1", "wd0", "down", "gd1", "d1a", "d1b", "gd0", "d0a", "d0b", "d1a", "d1b", "hb0", "d0a", "d0b", "hb1", "gu0",
-    "u0a", "u0b", "d1a", "gu1", "u1", "d0a", "u0a", "u0b", "fb0", "d1b", "d0b", "u1", "fb1", "d0a", "d1a", "ab0", "u0a", "d0b",
-    "ab3", "u0b", "d1b", "d1a", "gm", "m", "gh0", "d0a", "ab2", "d0b", "m", "d1b", "u1", "ab1", "u0a", "d1a", "gh3", "d0a", "u0b",
-    "last", "p", "d0b", "m", "u1", "d1b", "gh1", "h1a", "h1b", "d1a", "p", "u0a", "gh2", "h0a", "h0b", "d0a", "u0b", "h1a", "d0b",
-    "h1b", "d1a", "m", "h0a", "h0b", "vec", "v", "d0a", "d0b", "d1b", "u1", "v", "d1b", "u0a", "p", "u0b", "h1a", "h0a", "m",
-    "h1b", "h0b", "v", "u1", "h0a", "u0a", "p", "h0b", "u0a", "u0b", "m", "h1a", "v", "u0b", "h1b", "h0a", "p", "v", "h0b", "u1",
-    "h1a", "m", "u1", "h1b", "m", "h0a", "h0b", "p", "h1a", "h1b", "h0a", "p", "h0b", "h0a", "h1a", "h0b", "h1b", "h1a", "h1b",
+    "g0", "g1", "enter", "wm", "wd", "qkv0", "att0", "g0", "qkv1", "wu0", "g1", "att1", "wu1", "wm", "g0", "g1", "wd", "wm", "g0",
+    "wm", "g1", "wu0", "g0", "qkv2", "att2", "g1", "qkv3", "wd", "att3", "merge", "wu0", "up0", "wu1", "wd", "wu0", "wu1", "up1",
+    "wd", "down", "gd2", "d2", "gd3", "d3", "gd1", "d1", "d2", "gd0", "d0", "d3", "hb0", "d1", "d0", "hb1", "fb0", "d2", "d3",
+    "gu3", "u3", "gu1", "u1", "d1", "gu2", "u2", "u3", "gu0", "u0", "u1", "d2", "d0", "u2", "fb1", "u0", "d3", "d1", "gm", "m",
+    "ab0", "u3", "u1", "m", "ab2", "d2", "d0", "gh0", "u0", "u2", "gh2", "h0a", "h0b", "d3", "u3", "d1", "ab1", "h0a", "u1",
+    "h0b", "m", "u0", "u2", "ab3", "d1", "u3", "d2", "d0", "last", "p", "u1", "d3", "h0a", "h0b", "u2", "u0", "m", "d1", "d0",
+    "d2", "p", "u3", "gh3", "gh1", "h1a", "h1b", "d2", "h0a", "d3", "h0b", "u1", "vec", "v", "h1a", "h1b", "m", "d3", "u2", "d1",
+    "u0", "h0a", "d0", "u3", "v", "p", "h0b", "u1", "h1a", "h1b", "m", "d0", "u2", "d1", "h0a", "u1", "d1", "p", "u0", "h1b",
+    "u3", "h0b", "u0", "v", "h1a", "u2", "d0", "m", "h0a", "d0", "u1", "h0b", "h1a", "p", "u3", "h1b", "u1", "u2", "h0a", "v",
+    "m", "u3", "h1a", "u2", "h0b", "h1b", "m", "p", "v", "h0a", "m", "p", "h0a", "h1a", "h0b", "h1b", "h1a", "h0b", "h1b",
 )
 VMEM_LIMIT = 64 * 2**20 - 2**18
+POOL = 32
 HEAD = 64
 ROWS = 256
 NEG = -1000000000.0
@@ -65,7 +75,7 @@
 
 class Net:
     def __init__(self, send_sem, recv_sem, dp):
-        self.send_sem, self.recv_sem, self.sent, self.count = send_sem, recv_sem, [], 0
+        self.send_sem, self.recv_sem, self.slots, self.count = send_sem, recv_sem, [None] * POOL, 0
         i = lax.axis_index("dp")
         self.t = lax.axis_index("tensor")
         self.c = lax.rem(i, 2)
@@ -77,6 +87,9 @@
         self.zto = [lax.rem(self.z + s, 4) for s in range(1, 4)]
         self.zdev = [{"dp": i + 4 * (j - self.z)} for j in self.zto]
         self.zpair = {"dp": i + 4 * (1 - 2 * lax.rem(self.z, 2))}
+        self.zfar = {"dp": i + 4 * (3 - 2 * self.z)}
+        self.zb = self.z // 2
+        self.za = lax.rem(self.z, 2) + self.zb - 2 * lax.rem(self.z, 2) * self.zb
         self.e = lax.rem(i // 2, 8)
         self.eto = [lax.rem(self.e + s, 8) for s in range(1, 8)]
         self.edev = [{"dp": i + 2 * (j - self.e)} for j in self.eto]
@@ -89,7 +102,7 @@
             step *= 2
 
     def everyone(self):
-        more = ([self.xydev] if any("p" in o for *_, o in PIECES) else []) + (self.edev if any("8" in o for *_, o in PIECES) else [self.xdev] + self.zdev)
+        more = ([self.xydev] if any("p" in o or "q" in o for *_, o in PIECES) else []) + (self.edev if any("8" in o for *_, o in PIECES) else [self.xdev] + self.zdev)
         return [self.core, self.ydev] + more + self.extra
 
     def greet(self):
@@ -101,17 +114,27 @@
     def send(self, src, dst, device):
         k = self.count
         self.count += 1
+        slot = k % POOL
+        if self.slots[slot] is not None:
+            self.slots[slot].wait_send()
         copy = pltpu.make_async_remote_copy(
-            src_ref=src, dst_ref=dst, send_sem=self.send_sem.at[k], recv_sem=self.recv_sem.at[k],
+            src_ref=src, dst_ref=dst, send_sem=self.send_sem.at[slot], recv_sem=self.recv_sem.at[k],
             device_id=device, device_id_type=MESH,
         )
         copy.start()
-        self.sent.append(copy)
+        self.slots[slot] = copy
         return copy
 
+    def sent(self, copy):
+        for slot, other in enumerate(self.slots):
+            if other is copy:
+                copy.wait_send()
+                self.slots[slot] = None
+
     def finish(self):
-        for copy in self.sent:
-            copy.wait_send()
+        for copy in self.slots:
+            if copy is not None:
+                copy.wait_send()
 
 
 def tri(tb):
@@ -122,27 +145,27 @@
     return pl.ds(pl.multiple_of(base, size), size)
 
 
-def fetch_direct(net, ready, own, oth):
-    half = own.shape[0] // 2
+def fetch_direct(net, push, oth):
+    half = oth.shape[0] // 2
     r = part(net.c * half, half)
-    ready.wait()
-    y = net.send(own.at[r], oth.at[r], net.ydev)
-    yield
-    y.wait_recv()
+    ys = push(r)
+    yield
+    for y in ys:
+        y.wait_recv()
     c = net.send(oth.at[r], oth.at[r], net.core)
     yield
     c.wait_recv()
 
 
-def fetch_shared(net, ready, own, oth, along):
-    q = own.shape[0] // 4
+def fetch_shared(net, push, oth, along):
+    q = oth.shape[0] // 4
     bit, device = (net.x, net.xdev) if along == "x" else (lax.rem(net.z, 2), net.zpair)
     a = part((2 * net.c + bit) * q, q)
     b = part((2 * net.c + 1 - bit) * q, q)
-    ready.wait()
-    y = net.send(own.at[a], oth.at[a], net.ydev)
-    yield
-    y.wait_recv()
+    ys = push(a)
+    yield
+    for y in ys:
+        y.wait_recv()
     x = net.send(oth.at[a], oth.at[a], device)
     c0 = net.send(oth.at[a], oth.at[a], net.core)
     yield
@@ -151,6 +174,33 @@
     yield
     c0.wait_recv()
     c1.wait_recv()
+
+
+def fetch_plane(net, push, oth):
+    q = oth.shape[0] // 8
+    z = lax.rem(net.z, 2)
+    start = lambda x, z: (4 * net.c + 2 * x + z) * q
+    mine, by_x, by_z = start(net.x, z), start(1 - net.x, z), start(net.x, 1 - z)
+    ys = push(part(mine, q))
+    yield
+    for y in ys:
+        y.wait_recv()
+    again = lambda base, size, device: net.send(oth.at[part(base, size)], oth.at[part(base, size)], device)
+    x1, z1 = again(mine, q, net.xdev), again(mine, q, net.zpair)
+    cores = [again(mine, q, net.core)]
+    yield
+    x1.wait_recv()
+    z1.wait_recv()
+    z2 = again(by_x, q // 2, net.zpair)
+    x2 = again(by_z + q // 2, q // 2, net.xdev)
+    cores += [again(by_x, q, net.core), again(by_z, q, net.core)]
+    yield
+    x2.wait_recv()
+    z2.wait_recv()
+    cores.append(again(start(1 - net.x, 1 - z), q, net.core))
+    yield
+    for core in cores:
+        core.wait_recv()
 
 
 class Ready:
@@ -163,45 +213,66 @@
         self.copies = []
 
 
-def recv_rows(rows, order, extra):
-    size, halves, total = rows // 2, 2, rows
+def needs(rows, order, extra):
+    size, halves, both, one = rows // 2, 2, rows // 2, 0
+    copies = 2 + extra
     for stage in order:
-        if stage == "y":
-            total, halves = total + size, 1
-        elif stage == "x":
-            size //= 2
-            total += size * halves
-        elif stage == "z":
-            size //= 4
-            total += 3 * size * halves
-        elif stage == "8":
-            size //= 8
-            total += 7 * size * halves
-        elif stage == "p":
-            size //= 2
-            total, halves = total + 3 * size, 1
-    return total + extra * size
-
-
-def reduce(net, g, own, buf, fin, order):
+        count = {"x": 2, "a": 2, "b": 2, "z": 4, "8": 8}.get(stage, 1)
+        if stage in "pq":
+            size, halves = size // 2, 1
+            one += 3 * size
+            copies += 6 if stage == "p" else 4
+            copies += stage == "p"
+        elif stage == "y":
+            halves = 1
+            one += size
+            copies += 1
+        else:
+            size //= count
+            if halves == 2:
+                both += (count - 1) * size
+            else:
+                one += (count - 1) * size
+            copies += 2 * (count - 1)
+    return both, one + extra * size, copies
+
+
+class Arrival:
+    def __init__(self, copy):
+        self.copy, self.open = copy, True
+
+    def wait(self):
+        if self.open:
+            self.copy.wait_recv()
+        self.open = False
+
+
+def reduce(net, g, own, buf_both, buf_one, fin, order):
     rows = g.shape[1]
     oth = 1 - own
-    used = [0]
+    used = {2: 0, 1: 0}
     pending = {0: [], 1: []}
 
-    def take(k):
-        used[0] += k
-        return buf.at[used[0] - k : used[0]]
+    def take(k, halves=1):
+        used[halves] += k
+        rows = slice(used[halves] - k, used[halves])
+        return buf_both.at[:, rows] if halves == 2 else buf_one.at[rows]
+
+    def post_both(base, size, device):
+        dst = take(size, 2)
+        arrival = Arrival(net.send(g.at[:, part(base, size)], dst, device))
+        for h in (own, oth):
+            pending[h is oth].append((arrival, dst.at[h]))
 
     def post(h, base, size, device):
         dst = take(size)
-        pending[h is oth].append((net.send(g.at[h, part(base, size)], dst, device), dst))
+        pending[False].append((Arrival(net.send(g.at[h, part(base, size)], dst, device)), dst))
 
     def settle(h, base, size, to=None):
         here = part(base, size)
         total = g[h, here, :].astype(F32)
-        for copy, dst in pending[h is oth]:
-            copy.wait_recv()
+        for arrival, dst in pending[h is oth]:
+            arrival.wait()
             total = total + dst[...].astype(F32)
         pending[h is oth] = []
         if to is None:
@@ -211,36 +282,36 @@
 
     size = rows // 2
     base = net.c * size
-    halves = [oth, own]
-    for h in halves:
-        post(h, (1 - net.c) * size, size, net.core)
+    both = True
+    post_both((1 - net.c) * size, size, net.core)
     yield
     history = []
     for stage in order:
         history.append((stage, base, size))
+        if both:
+            settle(oth, base, size)
         if stage == "y":
-            settle(oth, base, size)
-            dst = take(size)
-            pending[False].append((net.send(g.at[oth, part(base, size)], dst, net.ydev), dst))
-            halves = [own]
-        elif stage == "p":
-            settle(oth, base, size)
+            post(oth, base, size, net.ydev)
+            both = False
+        elif stage in "pq":
             settle(own, base, size)
             size //= 2
             near, far = base + net.x * size, base + (1 - net.x) * size
-            for h, start, device in ((oth, far, net.xydev), (oth, near, net.ydev), (own, far, net.xdev)):
-                dst = take(size)
-                pending[False].append((net.send(g.at[h, part(start, size)], dst, device), dst))
-            base, halves = near, [own]
+            post(oth, far, size, net.xydev)
+            post(oth, near, size, net.ydev)
+            post(own, far, size, net.xdev)
+            base, both = near, False
         else:
-            for h in halves:
-                settle(h, base, size)
+            settle(own, base, size)
             count, to, devices, place = {"x": (2, [1 - net.x], [net.xdev], net.x), "z": (4, net.zto, net.zdev, net.z),
+                                         "a": (2, [1 - net.za], [net.zpair], net.za), "b": (2, [1 - net.zb], [net.zfar], net.zb),
                                          "8": (8, net.eto, net.edev, net.e)}[stage]
             size //= count
-            for h in halves:
-                for j, device in zip(to, devices):
-                    post(h, base + j * size, size, device)
+            for j, device in zip(to, devices):
+                if both:
+                    post_both(base + j * size, size, device)
+                else:
+                    post(own, base + j * size, size, device)
             base = base + place * size
         yield
     last = fin.at[own] if len(fin.shape) == 3 else fin
@@ -251,14 +322,14 @@
         copy = net.send(last.at[here], dst, device)
         yield
         copy.wait_recv()
-        copy.wait_send()
-        net.sent = [o for o in net.sent if o is not copy]
+        net.sent(copy)
         last[here, :] = (last[here, :].astype(F32) + dst[...].astype(F32)).astype(BF16)
     whole = [last]
     for stage, base, size in reversed(history):
         if stage == "y":
             continue
-        devices = {"x": [net.xdev], "z": net.zdev, "8": net.edev, "p": [net.xydev, net.ydev, net.xdev]}[stage]
+        devices = {"x": [net.xdev], "z": net.zdev, "a": [net.zpair], "b": [net.zfar], "8": net.edev, "q": [net.xdev],
+                   "p": [net.xydev, net.ydev, net.xdev]}[stage]
         copies = [net.send(last.at[here], last.at[here], device) for device in devices]
         yield
         for copy in copies:
@@ -357,27 +428,47 @@
     mb, g1, s1, db, g2, s2 = [vec[0, i : i + 1, :] for i in range(6)]
     vec_y = net.send(vec.at[0], vec.at[1], net.ydev)
 
+    def head_push(p):
+        def push(r):
+            return [
+                net.send(hw.at[c, r, p * C : (p + 1) * C], whp.at[1, p, r, c * C : (c + 1) * C], net.ydev) for c in range(3)
+            ]
+
+        return push
+
+    def row_push(own, oth, r0):
+        def push(r):
+            r = pl.ds(pl.multiple_of(r.start + r0, 16), r.size)
+            return [net.send(own.at[r], oth.at[r], net.ydev)]
+
+        return push
+
     steps = {}
-    halves = {"g0": (heads_in[0], whp.at[0, 0], whp.at[1, 0]), "g1": (heads_in[1], whp.at[0, 1], whp.at[1, 1])}
-    halves["wm"] = (merge_in, wm.at[0 : D // 2], wm.at[D // 2 :])
-    for k in range(2):
-        r = slice(k * D // 2, (k + 1) * D // 2)
-        halves[f"wu{k}"] = (up_in, wu.at[0, r], wu.at[1, r])
-        r = slice(k * FH // 2, (k + 1) * FH // 2)
-        halves[f"wd{k}"] = (down_in, wd.at[0, r], wd.at[1, r])
-    for name, way in FETCH:
-        steps[name] = fetch_direct(net, *halves[name]) if way == "y" else fetch_shared(net, *halves[name], way)
+    half = D // 2
+    weights = {"wm": (mw, wm.at[half : 2 * half]), "wu": (uw, wu.at[1]), "wd": (dw, wd.at[1])}
+    for name, key, r0, r1_, way in FETCH:
+        if key in weights:
+            own, oth = weights[key]
+            push, oth = row_push(own, oth, r0), oth.at[r0:r1_]
+        else:
+            push, oth = head_push(int(key[1])), whp.at[1, int(key[1])]
+        if way == "y":
+            steps[name] = fetch_direct(net, push, oth)
+        elif way == "e":
+            steps[name] = fetch_plane(net, push, oth)
+        else:
+            steps[name] = fetch_shared(net, push, oth, way)
     whole = {"m": (gm, fm, fm_h), "p": (gpos, fp, fp_h)}
     for k in range(2):
         whole[f"d{k}"] = (gd.at[k], fd.at[k], fd_h.at[k])
         whole[f"u{k}"] = (gu.at[k], fu.at[k], fu_h.at[k])
         whole[f"h{k}"] = (gh.at[k], fh.at[k], fh_h.at[k])
     ends = {"v": (vs.at[vs.shape[0] - 1], vg_h)}
-    for (name, key, r0, r1_, c0, c1, order), buf in zip(PIECES, bufs):
+    for (name, key, r0, r1_, c0, c1, order), buf_both, buf_one in zip(PIECES, bufs[::2], bufs[1::2]):
         g, f, f_h = whole[key]
         if key != "p":
             g, f, f_h = g.at[:, r0:r1_, c0:c1], f.at[r0:r1_, c0:c1], f_h.at[r0:r1_, c0:c1]
-        steps[name] = reduce(net, g, t_id if key == "p" else 0, buf, f, order)
+        steps[name] = reduce(net, g, t_id if key == "p" else 0, buf_both, buf_one, f, order)
         ends[name] = (f, f_h)
     steps["v"] = reduce_vectors(net, vs, vr, vz)
     def enter(j):
@@ -510,12 +601,16 @@
 
     def seg_down():
         cot_in.wait()
+        down_in.wait()
         loop(tiles // 2, down)
         move(cot, out_h)
 
-    def grad_down(c):
-        for h in (1, 0):
-            gd[c, h] = nn(bgt[...], hid[h, :, c * D : (c + 1) * D]).astype(BF16)
+    def quarter(grad, left, k):
+        n = FH // 4
+        cols = slice(k * n, (k + 1) * n)
+        ys = [nn(left[...], hid[h, :, cols]).astype(BF16) for h in (1, 0)]
+        for h, y in zip((1, 0), ys):
+            grad[k // 2, h, :, (k % 2) * n : (k % 2 + 1) * n] = y
 
     def hidden_back(j):
         rows = at(j, ROWS)
@@ -527,10 +622,6 @@
             hid[h, rows, c * D : (c + 1) * D] = vb[h, c]
         for h, c in todo:
             rowsum(3 + 2 * h + c, vb[h, c].astype(F32))
-
-    def grad_up(c):
-        for h in (1, 0):
-            gu[c, h] = nn(nbt[...], hid[h, :, c * D : (c + 1) * D]).astype(BF16)
 
     def first_back(jj):
         both = [at(2 * jj + i, ROWS) for i in range(2)]
@@ -633,16 +724,16 @@
         up(1)
 
     acc[...] = jnp.zeros_like(acc)
-    work = {"enter": seg_enter, "merge": lambda: loop(tiles // 2, merge), "up0": lambda: up(0), "up1": seg_up1, "down": seg_down}
+    work = {"enter": seg_enter, "merge": lambda: (merge_in.wait(), loop(tiles // 2, merge)), "up0": lambda: (up_in.wait(), up(0)), "up1": seg_up1, "down": seg_down}
     work.update({"gm": grad_merge, "vec": vectors, "last": seg_last})
     for p in range(4):
-        work[f"qkv{p}"] = lambda p=p: qkv(p // 2, p % 2)
+        work[f"gd{p}"] = lambda p=p: quarter(gd, bgt, p)
+        work[f"gu{p}"] = lambda p=p: quarter(gu, nbt, p)
+        work[f"qkv{p}"] = lambda p=p: (heads_in[p % 2].wait(), qkv(p // 2, p % 2))
         work[f"att{p}"] = lambda p=p: attend(p, range(W))
         work[f"ab{p}"] = lambda p=p: attend_back(p, range(W))
         work[f"gh{p}"] = lambda p=p: gh.__setitem__((p % 2, p // 2), nn(ait[...], dtrip[p]).astype(BF16))
     for k in range(2):
-        work[f"gd{k}"] = lambda k=k: grad_down(k)
-        work[f"gu{k}"] = lambda k=k: grad_up(k)
         work[f"hb{k}"] = lambda k=k: half(hidden_back, k)
         work[f"fb{k}"] = lambda k=k: first_back(k)
     for name in ORDER:
@@ -660,6 +751,7 @@
             pass
         if name in ends:
             move(*ends[name])
+    assert net.count <= recv_sem.shape[0], net.count
     net.finish()
     for copy in local[inward:]:
         copy.wait()
@@ -671,7 +763,14 @@
     area = strip(T // 128 - 1).stop
     X = max(1, (dp // 16).bit_length() - 1)
     NC, DH = FH // D, D // 2
-    sems = 240 + 40 * X
+    extra = (dp // 16).bit_length() - 1
+    bufs, copies = [], 7 + extra
+    for _, _, a, b, c, d, order in PIECES:
+        both, one, more = needs(b - a, order, extra)
+        bufs += [V((2, both, d - c), BF16), V((max(one, 16), d - c), BF16)]
+        copies += more
+    for _, key, _, _, way in FETCH:
+        copies += (3 if key[0] == "g" else 1) + {"y": 1, "x": 3, "z": 3, "e": 8}[way]
     assert NC == 2
     return [
         V((R, D), BF16), V((T, D), BF16), V((R, D), BF16), V((2, 2, D, 384), BF16), V((D, D), BF16), V((2, D, FH), BF16),
@@ -683,8 +782,8 @@
         V((NC, 2, D, D), BF16), V((NC, 2, D, D), BF16), V((2, DH, D), BF16), V((2, 2, D, 384), BF16), V((2, T // 2, D), BF16),
         V((NC, D, D), BF16), V((NC, D, D), BF16), V((DH, D), BF16), V((2, D, 384), BF16), V((2, T // 2, D), BF16),
         V((5 + (dp // 16).bit_length() - 1, 16, D), F32), V((3 + X, 16, D), F32), V((4, 16, D), F32),
-        pltpu.SemaphoreType.DMA((sems,)), pltpu.SemaphoreType.DMA((sems,)), pltpu.SemaphoreType.DMA((40,)),
-    ] + [V((recv_rows(b - a, order, (dp // 16).bit_length() - 1), d - c), BF16) for _, _, a, b, c, d, order in PIECES]
+        pltpu.SemaphoreType.DMA((POOL,)), pltpu.SemaphoreType.DMA((copies,)), pltpu.SemaphoreType.DMA((16 + len(PIECES),)),
+    ] + bufs
 
 
 def call(dp, tok, seg, pos, cot, hw, mw, uw, dw, *vecs):

time: 110 us -> 103 us (0.936)
  Pallas kernels: 109 us -> 102 us
    pallas_call x1, Pallas kernels: 102 us -> 95 us  [call(): pl.pallas_call(functools.partial(kernel, dp), out_shape=outs, in_specs=[h...]
where the time goes in v4:
time: 103 us
  Pallas kernels  102 us (99%)
    pallas_call x1, Pallas kernels, call(): pl.pallas_call(functools.partial(kernel, dp), out_shape=outs, in_specs=[h...  95 us
    pallas_call x1, Pallas kernels, finish(): pl.pallas_call(widen, out_shape=[S(out.shape, BF16), S(tg.shape, F32)] +...  6.99 us

profile of v4, /device:TPU:0, one launch (start us, length us, event | category | flops | bytes accessed | tf_op | source)
XLA Modules:
  0.0 102.8 jit_solution(12503278249374446104)
XLA Ops:
  0.7 95.0 %shard_map.254 = (bf16[1024,512]{1,0:T(8,128)(2,1)}, f32[1024,512]{1,0:T(8,128)}, bf16[2,512,512]{2,1,0:T(8,128)(2,1)}, bf16[2,512,512]{2,1,0:T(8,128)(2,1)}, bf...) custom-call(bf16[1024,512]{1,0:T(8,128)(2,1)} %tok_h.1, ...), custom_call_target="tpu_custom_call" | custom-call | tf_op jit(solution)/shard_map/pallas_call | solution.py:800
  95.7 7.0 %shard_map.255 = (bf16[1024,512]{1,0:T(8,128)(2,1)}, f32[1024,512]{1,0:T(8,128)}, f32[512,512]{1,0:T(8,128)}, f32[3,512,256]{2,1,0:T(8,128)}, f32[256,512]{1,0:T...) custom-call(bf16[1024,512]{1,0:T(8,128)(2,1)} %get-tuple-element.36., ...), custom_call_target="tpu_custom_call" | custom-call | tf_op jit(solution)/shard_map/pallas_call | solution.py:868
